TPU v7x, 32 devices: a whole 2x2x4 slice. The times are simulated.
32 devices in a mesh: shard: 8 (over y, x, core), rep: 4 (over z).
Axes of the slice: x: 2, y: 2, z: 4, core: 2. Of those that a mesh axis runs over, the one named last changes fastest.
Arguments:
- tokens: bfloat16 [16384, 1472], P(('shard', 'rep')), may hold values from -6 to 6
- cotangent: bfloat16 [16384, 1472], P(('shard', 'rep')), may hold values from -6 to 6
- buckets: int32 [1023], replicated, may hold values from 0 to 31
- bias_table: bfloat16 [32, 6], replicated, may hold values from -4 to 4
- attn_gain: bfloat16 [1472], P('shard'), may hold values from 0.25 to 1.75
- w_query: bfloat16 [1472, 384], P('shard'), may hold values from -0.0390625 to 0.0390625
- w_key: bfloat16 [1472, 384], P('shard'), may hold values from -0.15625 to 0.15625
- w_value: bfloat16 [1472, 384], P('shard'), may hold values from -0.15625 to 0.15625
- w_output: bfloat16 [1472, 384], P('shard'), may hold values from -1.25 to 1.25
- ffn_gain: bfloat16 [1472], P('shard'), may hold values from 0.25 to 1.75
- w_gate: bfloat16 [1472, 3584], P('shard'), may hold values from -0.15625 to 0.15625
- w_up: bfloat16 [1472, 3584], P('shard'), may hold values from -0.15625 to 0.15625
- w_down: bfloat16 [1472, 3584], P('shard'), may hold values from -0.09375 to 0.09375
Outputs:
- layer_out: bfloat16 [16384, 1472], P(('shard', 'rep'))
- grad_tokens: bfloat16 [16384, 1472], P(('shard', 'rep'))
- grad_attn_gain: float32 [1472], P('shard')
- grad_w_query: float32 [1472, 384], P('shard')
- grad_w_key: float32 [1472, 384], P('shard')
- grad_w_value: float32 [1472, 384], P('shard')
- grad_w_output: float32 [1472, 384], P('shard')
- grad_ffn_gain: float32 [1472], P('shard')
- grad_w_gate: float32 [1472, 3584], P('shard')
- grad_w_up: float32 [1472, 3584], P('shard')
- grad_w_down: float32 [1472, 3584], P('shard')
- grad_bias_table: float32 [32, 6], replicated
All inputs are finite; a program needn't handle non-finite values.
Results may differ from a plain program's by a relative error of at most 0.015.
The roundings to bfloat16 on the way count: a program that leaves them out, or rounds other values in their place, can miss the bound.
Values may be sent and summed in bfloat16 or wider, within the bound.
A program may use at most 320 MiB of HBM per device.

v0:
```python
import functools

import jax
import jax.numpy as jnp
from jax import lax
from jax.experimental import pallas as pl
from jax.experimental.pallas import tpu as pltpu
from jax.sharding import PartitionSpec as P

BLOCK = 256
MESH = pl.DeviceIdType.MESH
f32 = jnp.float32
bf16 = jnp.bfloat16


norm_eps = 1e-06
masked_score = -1e30
highest = lax.Precision.HIGHEST


def norm_local(row_values, gain_vector):
    return (
        row_values
        * lax.rsqrt(jnp.mean(row_values * row_values, axis=-1, keepdims=True) + norm_eps)
        * gain_vector
    )


def gelu_tanh(values_in):
    return jax.nn.gelu(values_in, approximate=True)


def diagonal_total(matrix):
    head_count, row_count, key_count = matrix.shape
    flipped = matrix[:, :, ::-1]
    padded = jnp.concatenate(
        [flipped, jnp.zeros((head_count, row_count, row_count), jnp.float32)], axis=2
    )
    flat_rows = padded.reshape(head_count, row_count * (key_count + row_count))
    flat_rows = flat_rows[:, : row_count * (key_count + row_count - 1)]
    return jnp.sum(flat_rows.reshape(head_count, row_count, key_count + row_count - 1), axis=1)


def toeplitz_grid(offset_bias, row_count, length):
    head_count = offset_bias.shape[0]
    span = length + row_count - 1
    flipped = offset_bias[:, ::-1]
    rotated = jnp.concatenate([flipped[:, row_count - 1 :], flipped[:, : row_count - 1]], axis=1)
    tiled = jnp.tile(rotated, (1, row_count))[:, : row_count * (span - 1)]
    return tiled.reshape(head_count, row_count, span - 1)[:, :, :length]


def body(
    tokens,
    cotangent,
    buckets,
    bias_table,
    attn_gain,
    w_query,
    w_key,
    w_value,
    w_output,
    ffn_gain,
    w_gate,
    w_up,
    w_down,
):
    length = tokens.shape[0]
    bucket_count = bias_table.shape[0]
    head_count = bias_table.shape[1]
    inner_width = w_query.shape[1]
    ff_width = w_gate.shape[1]
    owner_rows = w_query.shape[0]
    head_size = inner_width // head_count
    block_rows = min(512, length)
    block_count = length // block_rows
    residual = tokens.astype(jnp.float32)
    attn_set = (
        lax.all_gather(attn_gain, "shard", axis=0, tiled=True),
        lax.all_gather(w_query, "shard", axis=0, tiled=True),
        lax.all_gather(w_key, "shard", axis=0, tiled=True),
        lax.all_gather(w_value, "shard", axis=0, tiled=True),
        lax.all_gather(w_output, "shard", axis=0, tiled=True),
    )
    gain_one = attn_set[0].astype(jnp.float32)
    normed_one = norm_local(residual, gain_one).astype(jnp.bfloat16)

    def project(weight):
        product = jnp.dot(normed_one, weight, preferred_element_type=jnp.float32)
        return product.astype(jnp.bfloat16).reshape(length, head_count, head_size)

    queries = project(attn_set[1])
    key_rows = project(attn_set[2])
    value_rows = project(attn_set[3])
    one_hot = (buckets[:, None] == jnp.arange(bucket_count, dtype=jnp.int32)[None, :]).astype(
        jnp.float32
    )
    offset_bias = jnp.dot(one_hot, bias_table.astype(jnp.float32), precision=highest).T
    block_starts = jnp.arange(block_count, dtype=jnp.int32) * block_rows
    key_index = jnp.arange(length, dtype=jnp.int32)

    def block_scores(first_row, query_block):
        query_index = first_row + jnp.arange(block_rows, dtype=jnp.int32)
        bias_grid = toeplitz_grid(offset_bias, block_rows, length)
        scores = (
            jnp.einsum("qhd,khd->hqk", query_block, key_rows, preferred_element_type=jnp.float32)
            + bias_grid
        )
        allowed = key_index[None, :] // BLOCK <= query_index[:, None] // BLOCK
        return jnp.where(allowed[None], scores, masked_score)

    def attend(first_row):
        scores = block_scores(first_row, queries)
        row_max = jnp.max(scores, axis=-1, keepdims=True)
        exp_scores = jnp.exp(scores - row_max)
        totals = jnp.sum(exp_scores, axis=-1, keepdims=True)
        probability = (exp_scores / totals).astype(jnp.bfloat16)
        mixed_rows = jnp.einsum(
            "hqk,khd->qhd", probability, value_rows, preferred_element_type=jnp.float32
        )
        return (mixed_rows, (row_max + jnp.log(totals))[..., 0])

    mixed_blocks, log_totals = lax.map(attend, block_starts)
    attended = mixed_blocks.reshape(length, inner_width).astype(jnp.bfloat16)
    middle = residual + jnp.einsum(
        "ti,di->td", attended, attn_set[4], preferred_element_type=jnp.float32
    )
    ffn_set = (
        lax.all_gather(ffn_gain, "shard", axis=0, tiled=True),
        lax.all_gather(w_gate, "shard", axis=0, tiled=True),
        lax.all_gather(w_up, "shard", axis=0, tiled=True),
        lax.all_gather(w_down, "shard", axis=0, tiled=True),
    )
    gain_two = ffn_set[0].astype(jnp.float32)
    normed_two = norm_local(middle, gain_two).astype(jnp.bfloat16)
    gate_values = jnp.dot(normed_two, ffn_set[1], preferred_element_type=jnp.float32)
    up_values = jnp.dot(normed_two, ffn_set[2], preferred_element_type=jnp.float32)
    activated, gelu_pullback = jax.vjp(gelu_tanh, gate_values)
    hidden = (activated * up_values).astype(jnp.bfloat16)
    layer_out = (
        middle + jnp.einsum("tf,df->td", hidden, ffn_set[3], preferred_element_type=jnp.float32)
    ).astype(jnp.bfloat16)
    ffn_set = (
        lax.all_gather(ffn_gain, "shard", axis=0, tiled=True),
        lax.all_gather(w_gate, "shard", axis=0, tiled=True),
        lax.all_gather(w_up, "shard", axis=0, tiled=True),
        lax.all_gather(w_down, "shard", axis=0, tiled=True),
    )
    grad_w_down = jnp.einsum("td,tf->df", cotangent, hidden, preferred_element_type=jnp.float32)
    grad_hidden = jnp.dot(cotangent, ffn_set[3], preferred_element_type=jnp.float32)
    grad_gate = gelu_pullback(grad_hidden * up_values)[0].astype(jnp.bfloat16)
    grad_up = (grad_hidden * activated).astype(jnp.bfloat16)
    grad_w_gate = jnp.einsum("td,tf->df", normed_two, grad_gate, preferred_element_type=jnp.float32)
    grad_w_up = jnp.einsum("td,tf->df", normed_two, grad_up, preferred_element_type=jnp.float32)
    grad_normed_two = jnp.einsum(
        "tf,df->td", grad_gate, ffn_set[1], preferred_element_type=jnp.float32
    )
    grad_normed_two = grad_normed_two + jnp.einsum(
        "tf,df->td", grad_up, ffn_set[2], preferred_element_type=jnp.float32
    )
    middle_part, grad_gain_two = jax.vjp(norm_local, middle, gain_two)[1](grad_normed_two)
    grad_middle = cotangent.astype(jnp.float32) + middle_part
    ffn_shards = (
        lax.psum_scatter(grad_w_gate.astype(jnp.bfloat16), "shard", scatter_dimension=0, tiled=True),
        lax.psum_scatter(grad_w_up.astype(jnp.bfloat16), "shard", scatter_dimension=0, tiled=True),
        lax.psum_scatter(grad_w_down.astype(jnp.bfloat16), "shard", scatter_dimension=0, tiled=True),
    )
    attn_set = (
        lax.all_gather(attn_gain, "shard", axis=0, tiled=True),
        lax.all_gather(w_query, "shard", axis=0, tiled=True),
        lax.all_gather(w_key, "shard", axis=0, tiled=True),
        lax.all_gather(w_value, "shard", axis=0, tiled=True),
        lax.all_gather(w_output, "shard", axis=0, tiled=True),
    )
    grad_branch = grad_middle.astype(jnp.bfloat16)
    grad_w_output = jnp.einsum(
        "td,ti->di", grad_branch, attended, preferred_element_type=jnp.float32
    )
    grad_attended = jnp.einsum(
        "td,di->ti", grad_branch, attn_set[4], preferred_element_type=jnp.float32
    )
    grad_attended = grad_attended.astype(jnp.bfloat16).reshape(length, head_count, head_size)

    def attend_back(carried, block_input):
        grad_keys, grad_values, grad_offsets = carried
        first_row, log_total = block_input
        scores = block_scores(first_row, queries)
        probability = jnp.exp(scores - log_total[..., None])
        grad_probs = jnp.einsum(
            "qhd,khd->hqk", grad_attended, value_rows, preferred_element_type=jnp.float32
        )
        inner_sum = jnp.sum(probability * grad_probs, axis=-1, keepdims=True)
        grad_scores = (probability * (grad_probs - inner_sum)).astype(jnp.bfloat16)
        grad_values = grad_values + jnp.einsum(
            "hqk,qhd->khd",
            probability.astype(jnp.bfloat16),
            grad_attended,
            preferred_element_type=jnp.float32,
        )
        grad_keys = grad_keys + jnp.einsum(
            "hqk,qhd->khd", grad_scores, queries, preferred_element_type=jnp.float32
        )
        grad_queries = jnp.einsum(
            "hqk,khd->qhd", grad_scores, key_rows, preferred_element_type=jnp.float32
        )
        diagonal_sums = diagonal_total(grad_scores.astype(jnp.float32))
        offset_piece = grad_offsets
        grad_offsets = offset_piece + diagonal_sums
        return ((grad_keys, grad_values, grad_offsets), grad_queries)

    zero_rows = jnp.zeros((length, head_count, head_size), jnp.float32)
    zero_offsets = jnp.zeros((head_count, 2 * length - 1), jnp.float32)
    (grad_keys, grad_values, grad_offsets), query_blocks = lax.scan(
        attend_back, (zero_rows, zero_rows, zero_offsets), (block_starts, log_totals)
    )
    grad_queries = query_blocks.reshape(length, inner_width).astype(jnp.bfloat16)
    grad_keys = grad_keys.reshape(length, inner_width).astype(jnp.bfloat16)
    grad_values = grad_values.reshape(length, inner_width).astype(jnp.bfloat16)
    grad_w_query = jnp.einsum(
        "td,ti->di", normed_one, grad_queries, preferred_element_type=jnp.float32
    )
    grad_w_key = jnp.einsum("td,ti->di", normed_one, grad_keys, preferred_element_type=jnp.float32)
    grad_w_value = jnp.einsum(
        "td,ti->di", normed_one, grad_values, preferred_element_type=jnp.float32
    )
    grad_normed_one = jnp.einsum(
        "ti,di->td", grad_queries, attn_set[1], preferred_element_type=jnp.float32
    )
    grad_normed_one = grad_normed_one + jnp.einsum(
        "ti,di->td", grad_keys, attn_set[2], preferred_element_type=jnp.float32
    )
    grad_normed_one = grad_normed_one + jnp.einsum(
        "ti,di->td", grad_values, attn_set[3], preferred_element_type=jnp.float32
    )
    rows_part, grad_gain_one = jax.vjp(norm_local, residual, gain_one)[1](grad_normed_one)
    grad_tokens = (grad_middle + rows_part).astype(jnp.bfloat16)
    grad_table = jnp.dot(grad_offsets, one_hot, precision=highest).T
    owner_start = lax.axis_index("shard") * owner_rows
    attn_shards = (
        lax.psum_scatter(grad_w_query.astype(jnp.bfloat16), "shard", scatter_dimension=0, tiled=True),
        lax.psum_scatter(grad_w_key.astype(jnp.bfloat16), "shard", scatter_dimension=0, tiled=True),
        lax.psum_scatter(grad_w_value.astype(jnp.bfloat16), "shard", scatter_dimension=0, tiled=True),
        lax.psum_scatter(grad_w_output.astype(jnp.bfloat16), "shard", scatter_dimension=0, tiled=True),
    )
    summed = lax.psum(
        (
            attn_shards[0],
            attn_shards[1],
            attn_shards[2],
            attn_shards[3],
            ffn_shards[0],
            ffn_shards[1],
            ffn_shards[2],
        ),
        "rep",
    )
    small_total = lax.psum((grad_gain_one, grad_gain_two, grad_table), ("shard", "rep"))
    gain_one_own = lax.dynamic_slice_in_dim(small_total[0], owner_start, owner_rows, 0)
    gain_two_own = lax.dynamic_slice_in_dim(small_total[1], owner_start, owner_rows, 0)
    return (
        layer_out,
        grad_tokens,
        gain_one_own,
        summed[0].astype(jnp.float32),
        summed[1].astype(jnp.float32),
        summed[2].astype(jnp.float32),
        summed[3].astype(jnp.float32),
        gain_two_own,
        summed[4].astype(jnp.float32),
        summed[5].astype(jnp.float32),
        summed[6].astype(jnp.float32),
        small_total[2],
    )


def dot_nn(a, b):
    return lax.dot_general(a, b, (((1,), (0,)), ((), ())), preferred_element_type=f32)


def dot_nt(a, b):
    return lax.dot_general(a, b, (((1,), (1,)), ((), ())), preferred_element_type=f32)


def dot_tn(a, b):
    return lax.dot_general(a, b, (((0,), (0,)), ((), ())), preferred_element_type=f32)


def fused_kernel(
    xt_ref,
    ct_ref,
    buckets_ref,
    table_ref,
    gains_ref,
    wq_ref,
    wk_ref,
    wv_ref,
    wo_ref,
    wg_ref,
    wu_ref,
    wd_ref,
    out_ref,
    gtok_ref,
    small_ref,
    gq_ref,
    gk_ref,
    gv_ref,
    go_ref,
    gg_ref,
    gu_ref,
    gd_ref,
    land_ref,
    gland,
    gcol,
    n1t,
    n2t,
    mid,
    acc_o,
    acc_n,
    qt,
    kt,
    vt,
    att,
    dat,
    dqt,
    dkt,
    dvt,
    wq,
    wk,
    wv,
    wo,
    wg2,
    wu2,
    wd2,
    wload,
    g,
    hid,
    dgt,
    dup,
    rc,
    rxy,
    r2,
    vbuf,
    zi,
    zm,
    ubuf,
    revb,
    onehot,
    doff,
    sms,
    smr,
    gain_s,
    gain_r,
    gsend,
    gloc,
    g1r,
    g2r,
    gpr,
    load_sem,
    e0s,
    e0r,
    e1s,
    e1r,
    e2s,
    e2r,
    zis,
    zir,
    zms,
    zmr,
    us,
    ul,
    ur,
    sss,
    ssr,
    zcredit,
    *,
    chunks,
    heads,
):
    width = xt_ref.shape[0]
    toks = xt_ref.shape[1]
    rows = gains_ref.shape[0]
    fw = land_ref.shape[3]
    sub = fw // 3
    aw = wq_ref.shape[1]
    hs = aw // heads
    total = chunks + 2
    eps = 1e-06
    lanes = revb.shape[1]
    big = 2 * rows
    nbig = width // big

    s = lax.axis_index("shard")
    r = lax.axis_index("rep")
    c = s % 2
    x = (s // 2) % 2
    y = s // 4
    sc = s + 1 - 2 * c
    sx = s + 2 - 4 * x
    sy = s + 4 - 8 * y
    bx = sx - c
    by = sy - c
    bd = (1 - y) * 4 + (1 - x) * 2
    b_own = s - c
    mate = r + 1 - 2 * (r % 2)
    inner = (r == 1) | (r == 2)
    outer = (r == 0) | (r == 3)

    def remote(src, dst, ssem, rsem, dev):
        return pltpu.make_async_remote_copy(
            src_ref=src, dst_ref=dst, send_sem=ssem, recv_sem=rsem, device_id=dev, device_id_type=MESH
        )

    def settle(ref, sem):
        pltpu.make_async_copy(ref, ref, sem).wait()

    barrier = pltpu.get_barrier_semaphore()
    near = [(sc, r), (bx, r), (bx + 1, r), (by, r), (by + 1, r), (bd, r), (bd + 1, r), (s, mate), (sc, mate)]
    for dev in near:
        pl.semaphore_signal(barrier, inc=1, device_id=dev, device_id_type=MESH)

    @pl.when(inner)
    def _():
        pl.semaphore_signal(barrier, inc=1, device_id=(s, 3 - r), device_id_type=MESH)

    @pl.when(inner)
    def _():
        pl.semaphore_wait(barrier, len(near) + 1)

    @pl.when(outer)
    def _():
        pl.semaphore_wait(barrier, len(near))

    def place(chunk, index):
        kind, k = chunk
        if kind == "a":
            return g.at[16 + index, :, pl.ds(k * aw, aw)]
        return land_ref.at[k, index]

    def places(chunk, count):
        kind, k = chunk
        if kind == "a":
            return g.at[pl.ds(16, count), :, pl.ds(k * aw, aw)]
        return land_ref.at[k, pl.ds(0, count)]

    def columns(k, half):
        return pl.ds(pl.multiple_of((2 * k + half) * sub, sub), sub)

    def own_parts(chunk, half):
        kind, k = chunk
        dst = place(chunk, half * 8 + s)
        if kind == "a":
            return [(((wq_ref, wk_ref), (wv_ref, wo_ref))[k][half], dst)]
        return [
            (ref.at[:, columns(k, half)], dst.at[:, pl.ds(j * sub, sub)]) for j, ref in enumerate((wg_ref, wu_ref, wd_ref))
        ]

    def at(chunk):
        kind, k = chunk
        return k if kind == "a" else k + 2

    def gather_send(chunk):
        i = at(chunk)
        for half in (0, 1):
            for src, dst in own_parts(chunk, half):
                remote(src, dst, gsend.at[i], g1r.at[i], (bx + half, r)).start()
                remote(src, dst, gsend.at[i], g1r.at[i], (by + half, r)).start()
        for half in (0, 1):
            for src, dst in own_parts(chunk, half):
                remote(src, dst, gsend.at[i], gpr.at[i], (sc, r)).start()
                pltpu.make_async_copy(src, dst, gloc.at[i]).start()

    def gather_forward(chunk):
        i = at(chunk)
        settle(places(chunk, 4), g1r.at[i])
        one = place(chunk, c * 8 + bx)
        two = place(chunk, c * 8 + by + 1)
        remote(one, one, gsend.at[i], g2r.at[i], (sy, r)).start()
        remote(two, two, gsend.at[i], g2r.at[i], (sx, r)).start()
        for b in (bx, bx + 1, by, by + 1):
            spot = place(chunk, c * 8 + b)
            remote(spot, spot, gsend.at[i], gpr.at[i], (sc, r)).start()

    def gather_swap(chunk):
        i = at(chunk)
        settle(places(chunk, 2), g2r.at[i])
        for b in (bd, bd + 1):
            spot = place(chunk, c * 8 + b)
            remote(spot, spot, gsend.at[i], gpr.at[i], (sc, r)).start()

    def gather_done(chunk):
        i = at(chunk)
        settle(places(chunk, 8), gpr.at[i])
        settle(places(chunk, 2), gloc.at[i])

    def gather_sent(chunk):
        settle(places(chunk, 14), gsend.at[at(chunk)])

    def cut(ref, w):
        return ref if w == fw else ref.at[:, :, pl.ds(0, w)]

    def cut1(ref, index, w):
        return ref.at[index] if w == fw else ref.at[index, :, pl.ds(0, w)]

    def span(ref, start, count, w):
        return ref.at[pl.ds(start, count)] if w == fw else ref.at[pl.ds(start, count), :, pl.ds(0, w)]

    def get(ref, index, w):
        return ref[index] if w == fw else ref[index, :, 0:w]

    def put(ref, index, w, value):
        if w == fw:
            ref[index] = value
        else:
            ref[index, :, 0:w] = value

    def add_to(dst, i, src, j, w):
        value = get(dst, i, w).astype(f32) + get(src, j, w).astype(f32)
        put(dst, i, w, value.astype(bf16))

    def core_send(n, w):
        slot = n % 2
        remote(
            span(g, slot * 16 + (1 - c) * 8, 8, w), span(rc, slot * 8, 8, w), e0s.at[n], e0r.at[n], (sc, r)
        ).start()

    def plane_send(n, w):
        slot = n % 2
        base = slot * 16 + c * 8
        settle(span(rc, slot * 8, 8, w), e0r.at[n])

        @pl.loop(0, 8)
        def _(b):
            add_to(g, base + b, rc, slot * 8 + b, w)

        for k in (0, 1):
            remote(
                cut1(g, base + 4 * k + 2 * (1 - x), w), cut1(rxy, slot * 4 + k, w), e1s.at[n], e1r.at[n], (sx, r)
            ).start()
            remote(
                cut1(g, base + 4 * (1 - y) + 2 * k + 1, w),
                cut1(rxy, slot * 4 + 2 + k, w),
                e1s.at[n],
                e1r.at[n],
                (sy, r),
            ).start()

    def plane_turn(n, w):
        slot = n % 2
        base = slot * 16 + c * 8
        settle(span(rxy, slot * 4, 4, w), e1r.at[n])
        first = base + 4 * (1 - y) + 2 * x
        second = base + 4 * y + 2 * (1 - x) + 1
        mine = base + b_own
        add_to(g, first, rxy, slot * 4 + 1 - y, w)
        add_to(g, second, rxy, slot * 4 + 2 + 1 - x, w)
        add_to(g, mine, rxy, slot * 4 + y, w)
        add_to(g, mine + 1, rxy, slot * 4 + 2 + x, w)
        remote(cut1(g, first, w), cut1(r2, slot * 2, w), e2s.at[n], e2r.at[n], (sy, r)).start()
        remote(cut1(g, second, w), cut1(r2, slot * 2 + 1, w), e2s.at[n], e2r.at[n], (sx, r)).start()

    def rep_send(n, w):
        slot = n % 2
        base = slot * 16 + c * 8
        settle(span(r2, slot * 2, 2, w), e2r.at[n])
        if isinstance(n, int):
            if n >= 2:
                pl.when(outer)(functools.partial(rep_free, n))
        else:
            pl.when(outer & (n >= 2))(functools.partial(rep_free, n))
        for j in (0, 1):
            value = get(g, base + b_own + j, w).astype(f32) + get(r2, slot * 2 + j, w).astype(f32)
            put(vbuf, slot * 2 + j, w, value.astype(bf16))

        @pl.when(outer)
        def _():
            remote(
                span(vbuf, slot * 2, 2, w), span(zi, slot * 2, 2, w), zis.at[n], zir.at[n], (s, mate)
            ).start()

        settle(span(g, slot * 16, 8, w), e0s.at[n])
        settle(span(rxy, slot * 4, 4, w), e1s.at[n])
        settle(span(r2, slot * 2, 2, w), e2s.at[n])

    def width_of(n):
        return fw if not isinstance(n, int) or n < chunks else aw

    def rep_free(n):
        earlier = n - 2
        slot = n % 2
        settle(span(vbuf, slot * 2, 2, width_of(earlier)), zis.at[earlier])
        pl.semaphore_wait(zcredit, 1)

    def rep_turn(n, w):
        slot = n % 2

        @pl.when(inner)
        def _():
            settle(span(zi, slot * 2, 2, w), zir.at[n])
            for j in (0, 1):
                add_to(vbuf, slot * 2 + j, zi, slot * 2 + j, w)

            def credit():
                pl.semaphore_signal(zcredit, inc=1, device_id=(s, mate), device_id_type=MESH)

            if isinstance(n, int):
                if n + 2 < total:
                    credit()
            else:
                credit()
            remote(
                span(vbuf, slot * 2, 2, w), span(zm, slot * 2, 2, w), zms.at[n], zmr.at[n], (s, 3 - r)
            ).start()

    def result(n, half, block):
        if isinstance(n, int) and n >= chunks:
            return [(block, ((gv_ref, go_ref), (gq_ref, gk_ref))[n - chunks][half])]
        return [
            (block.at[:, pl.ds(j * sub, sub)], ref.at[:, columns(n, half)])
            for j, ref in enumerate((gg_ref, gu_ref, gd_ref))
        ]

    def u_free(n, w):
        slot = n % 2
        for k in (0, 1, 2):
            settle(cut1(ubuf, slot * 2, w), us.at[n, k])
        settle(cut1(ubuf, slot * 2, w), ul.at[n])

    def rep_last(n, w):
        slot = n % 2

        @pl.when(inner)
        def _():
            settle(span(zm, slot * 2, 2, w), zmr.at[n])
            if isinstance(n, int):
                if n >= 2:
                    u_free(n - 2, width_of(n - 2))
            else:
                pl.when(n >= 2)(lambda: u_free(n - 2, w))
            for j in (0, 1):
                value = get(vbuf, slot * 2 + j, w).astype(f32) + get(zm, slot * 2 + j, w).astype(f32)
                put(ubuf, slot * 2 + j, w, value.astype(bf16))
            keep = cut1(ubuf, slot * 2 + c, w)
            give = cut1(ubuf, slot * 2 + 1 - c, w)

            def finish(half):
                for src, dst in result(n, half, keep):
                    remote(src, dst, us.at[n, 0], ur.at[n, half], (s, mate)).start()
                    pltpu.make_async_copy(src, dst, ul.at[n]).start()
                for src, dst in result(n, half, give):
                    remote(src, dst, us.at[n, 1], ur.at[n, half], (sc, mate)).start()
                    remote(src, dst, us.at[n, 2], ur.at[n, half], (sc, r)).start()

            if w == fw:
                finish(c)
            else:
                pl.when(c == 0)(lambda: finish(0))
                pl.when(c == 1)(lambda: finish(1))
            settle(span(vbuf, slot * 2, 2, w), zms.at[n])

    def small_send(step):
        if step < 3:
            dev = ((sc, r), (sx, r), (sy, r))[step]
            remote(sms.at[step], smr.at[step], sss.at[step], ssr.at[step], dev).start()
        elif step == 3:

            @pl.when(outer)
            def _():
                remote(sms.at[3], smr.at[3], sss.at[3], ssr.at[3], (s, mate)).start()
        elif step == 4:

            @pl.when(inner)
            def _():
                remote(sms.at[4], smr.at[4], sss.at[4], ssr.at[4], (s, 3 - r)).start()
        else:

            @pl.when(inner)
            def _():
                remote(sms.at[5], smr.at[5], sss.at[5], ssr.at[5], (s, mate)).start()

    def small_step(step):
        def take():
            settle(smr.at[step], ssr.at[step])
            settle(sms.at[step], sss.at[step])
            if step < 2:
                sms[step + 1] = sms[step] + smr[step]
            elif step == 2:
                sms[3] = sms[2] + smr[2]

        if step < 3:
            take()
            small_send(step + 1)
        elif step == 3:

            @pl.when(inner)
            def _():
                settle(smr.at[3], ssr.at[3])
                sms[4] = sms[3] + smr[3]

            @pl.when(outer)
            def _():
                settle(sms.at[3], sss.at[3])

            small_send(4)
        elif step == 4:

            @pl.when(inner)
            def _():
                settle(smr.at[4], ssr.at[4])
                settle(sms.at[4], sss.at[4])
                sms[5] = sms[4] + smr[4]
                small_ref[...] = sms[5]

            small_send(5)
        else:

            @pl.when(inner)
            def _():
                settle(sms.at[5], sss.at[5])

            @pl.when(outer)
            def _():
                settle(smr.at[5], ssr.at[5])
                small_ref[...] = smr[5]

    tile = 64
    tiles = width // tile

    def over_rows(body, start):
        def step(i, carry):
            return body(pl.ds(pl.multiple_of(i * tile, tile), tile), carry)

        return lax.fori_loop(0, tiles, step, start)

    def fold(value):
        return jnp.sum(value.reshape(tile // 8, 8, toks), axis=0)

    zero8 = jnp.zeros((8, toks), f32)

    gather_send(("a", 0))
    gdst = gland.at[s]
    for k, dev in enumerate([(sc, r), (bx, r), (bx + 1, r), (by, r), (by + 1, r), (bd, r), (bd + 1, r)]):
        remote(gains_ref, gdst, gain_s, gain_r, dev).start()
    pltpu.make_async_copy(gains_ref, gdst, load_sem.at[1]).start()
    gather_send(("a", 1))
    gather_send(("f", 0))

    def square_sum(sl, acc):
        v = xt_ref[sl, :].astype(f32)
        return acc + fold(v * v)

    ssum = jnp.sum(over_rows(square_sum, zero8), axis=0, keepdims=True)
    r1 = lax.rsqrt(ssum * (1.0 / width) + eps)

    bucket_index = lax.broadcasted_iota(jnp.int32, (table_ref.shape[1], lanes), 0)
    rev_hot = (bucket_index == buckets_ref[0:1, :]).astype(bf16)
    onehot[...] = (bucket_index == buckets_ref[1:2, :]).astype(bf16)
    revb[...] = dot_nn(table_ref[...], rev_hot)

    settle(gland.at[pl.ds(0, 7)], gain_r)
    settle(gland.at[0], load_sem.at[1])
    for b in range(8):
        gcol[rows * b : rows * (b + 1), :] = gland[b].astype(f32)

    def norm_one(sl, carry):
        v = xt_ref[sl, :].astype(f32)
        n1t[sl, :] = (v * r1 * gcol[sl, 0:1]).astype(bf16)
        return carry

    gather_forward(("a", 0))
    over_rows(norm_one, 0)
    gather_swap(("a", 0))
    gather_forward(("a", 1))
    gather_send(("f", 1))

    def compact(dst, half, col):
        @pl.loop(0, nbig)
        def _(i):
            both = jnp.concatenate(
                [
                    g[16 + half * 8 + 2 * i, :, col : col + aw].astype(f32),
                    g[16 + half * 8 + 2 * i + 1, :, col : col + aw].astype(f32),
                ],
                axis=0,
            )
            dst[pl.ds(pl.multiple_of(i * 2 * rows, 16), 2 * rows), :] = both.astype(bf16)

    gather_done(("a", 0))
    compact(wq, 0, 0)
    qt[...] = dot_tn(wq[...], n1t[...]).astype(bf16)
    compact(wk, 1, 0)
    kt[...] = dot_tn(wk[...], n1t[...]).astype(bf16)
    gather_swap(("a", 1))
    gather_done(("a", 1))
    compact(wv, 0, aw)
    vt[...] = dot_tn(wv[...], n1t[...]).astype(bf16)
    compact(wo, 1, aw)
    gather_forward(("f", 0))
    gather_send(("f", 2))

    half_tok = toks // 2

    def softmax_block(h, head, block):
        keys = half_tok * (block + 1)
        low = half_tok * block
        row = jnp.broadcast_to(revb[pl.ds(h, 1), :], (half_tok, lanes))
        bias = pltpu.roll(row, (low + 1 - toks) % lanes, 1, stride=1, stride_axis=0)[:, :keys]
        scores = dot_tn(qt[head, low : low + half_tok], kt[head, 0:keys]) + bias
        e = jnp.exp(scores - jnp.max(scores, axis=1, keepdims=True))
        return e * (1.0 / jnp.sum(e, axis=1, keepdims=True)), low, keys

    def attend(h, carry):
        head = pl.ds(pl.multiple_of(h * hs, hs), hs)
        for block in (0, 1):
            p, low, keys = softmax_block(h, head, block)
            att[head, low : low + half_tok] = dot_nt(vt[head, 0:keys], p.astype(bf16)).astype(bf16)
        return carry

    lax.fori_loop(0, heads // 2, attend, 0)
    gather_swap(("f", 0))
    gather_forward(("f", 1))
    lax.fori_loop(heads // 2, heads, attend, 0)

    def branch_one(i, acc):
        sl = pl.ds(pl.multiple_of(i * big, 16), big)
        m = xt_ref[sl, :].astype(f32) + dot_nn(wo[sl, :], att[...])
        mid[sl, :] = m
        return acc + jnp.sum((m * m).reshape(big // 8, 8, toks), axis=0)

    ssum = jnp.sum(lax.fori_loop(0, nbig, branch_one, zero8), axis=0, keepdims=True)
    r2n = lax.rsqrt(ssum * (1.0 / width) + eps)

    def norm_two(sl, carry):
        m = mid[sl, :]
        n2t[sl, :] = (m * r2n * gcol[sl, 1:2]).astype(bf16)
        acc_o[sl, :] = m
        acc_n[sl, :] = jnp.zeros((tile, toks), f32)
        return carry

    over_rows(norm_two, 0)

    tok_tile = toks // 2

    def ffn_chunk(t):
        slot = t % 2
        parts = [(half, k) for half in (0, 1) for k in (0, 1, 2)]

        def load(p):
            half, k = parts[p]
            return pltpu.make_async_copy(
                land_ref.at[t, pl.ds(half * 8, 8), :, pl.ds(k * sub, sub)],
                wload.at[pl.ds((p % 2) * 8, 8)],
                load_sem.at[p % 2],
            )

        load(0).start()
        for p, (half, k) in enumerate(parts):
            if p + 1 < len(parts):
                load(p + 1).start()
            load(p).wait()
            dst = (wg2, wu2, wd2)[k]

            @pl.loop(0, nbig)
            def _(i):
                base = (p % 2) * 8 + 2 * i
                both = jnp.concatenate([wload[base].astype(f32), wload[base + 1].astype(f32)], axis=0)
                sl = pl.ds(pl.multiple_of(i * big, 16), big)
                dst[sl, half * sub : (half + 1) * sub] = both.astype(bf16)

        @pl.loop(0, toks // tok_tile)
        def _(m):
            sl = pl.ds(pl.multiple_of(m * tok_tile, tok_tile), tok_tile)
            gate = dot_tn(n2t[:, sl], wg2[...])
            up = dot_tn(n2t[:, sl], wu2[...])
            gh = dot_tn(ct_ref[:, sl], wd2[...])
            k0 = 0.7978845608028654
            k1 = 0.044715
            sq = gate * gate
            th = jnp.tanh(k0 * (gate + k1 * (sq * gate)))
            half_one = 0.5 * (1.0 + th)
            act = gate * half_one
            slope = half_one + 0.5 * gate * (1.0 - th * th) * (k0 * (1.0 + 3.0 * k1 * sq))
            hid[sl, :] = (act * up).astype(bf16)
            dgt[sl, :] = (gh * up * slope).astype(bf16)
            dup[sl, :] = (gh * act).astype(bf16)

        @pl.loop(0, nbig)
        def _(i):
            sl = pl.ds(pl.multiple_of(i * big, 16), big)
            acc_o[sl, :] += dot_nt(wd2[sl, :], hid[...])
            acc_n[sl, :] += dot_nt(wg2[sl, :], dgt[...]) + dot_nt(wu2[sl, :], dup[...])
            for k, value in enumerate(
                (dot_nn(n2t[sl, :], dgt[...]), dot_nn(n2t[sl, :], dup[...]), dot_nn(ct_ref[sl, :], hid[...]))
            ):
                for half in (0, 1):
                    for j in (0, 1):
                        g[slot * 16 + half * 8 + 2 * i + j, :, k * sub : (k + 1) * sub] = value[
                            rows * j : rows * (j + 1), half * sub : (half + 1) * sub
                        ].astype(bf16)

    def ffn_step(t, carry):
        pl.when(t + 1 < chunks)(lambda: gather_swap(("f", t + 1)))
        pl.when(t + 2 < chunks)(lambda: gather_forward(("f", t + 2)))
        pl.when(t + 3 < chunks)(lambda: gather_send(("f", t + 3)))
        pl.when(t >= 3)(lambda: rep_turn(t - 3, fw))
        pl.when(t >= 2)(lambda: rep_send(t - 2, fw))
        gather_done(("f", t))
        ffn_chunk(t)
        core_send(t, fw)
        pl.when(t >= 3)(lambda: rep_last(t - 3, fw))
        pl.when(t >= 1)(lambda: plane_turn(t - 1, fw))
        plane_send(t, fw)
        return carry

    gather_sent(("a", 0))
    gather_sent(("a", 1))
    lax.fori_loop(0, chunks, ffn_step, 0)

    nv = chunks
    nq = chunks + 1
    rep_turn(nv - 3, fw)
    rep_send(nv - 2, fw)
    pick = lax.broadcasted_iota(jnp.int32, (8, toks), 0)

    def token_sums(row):
        chosen = (pick == row).astype(bf16)
        return dot_nt(chosen, wg2[...]) + dot_nt(chosen, wu2[...])

    def second_mean(sl, acc):
        return acc + fold(gcol[sl, 1:2] * acc_n[sl, :] * mid[sl, :])

    back = jnp.sum(over_rows(second_mean, zero8), axis=0, keepdims=True) * (1.0 / width)
    back = back * (r2n * r2n * r2n)

    def second_norm(sl, carry):
        m = mid[sl, :]
        gn = acc_n[sl, :]
        out_ref[sl, :] = acc_o[sl, :].astype(bf16)
        v = gn * m * r2n
        hi = v.astype(bf16)
        wg2[sl, :] = hi
        wu2[sl, :] = (v - hi.astype(f32)).astype(bf16)
        gm = ct_ref[sl, :].astype(f32) + r2n * gcol[sl, 1:2] * gn - m * back
        acc_n[sl, :] = gm
        n2t[sl, :] = gm.astype(bf16)
        return carry

    over_rows(second_norm, 0)
    sms[0] = jnp.zeros(sms.shape[1:], f32)
    sms[0, :, 0:width] = token_sums(1)
    rep_last(nv - 3, fw)
    plane_turn(nv - 1, fw)

    dat[...] = dot_tn(wo[...], n2t[...]).astype(bf16)

    def weight_grad(n, half, left, right):
        @pl.loop(0, nbig)
        def _(i):
            sl = pl.ds(pl.multiple_of(i * big, 16), big)
            value = dot_nt(left[sl, :], right[...])
            for j in (0, 1):
                g[(n % 2) * 16 + half * 8 + 2 * i + j, :, 0:aw] = value[rows * j : rows * (j + 1), :].astype(bf16)

    weight_grad(nv, 1, n2t, att)
    flip = (
        lax.broadcasted_iota(jnp.int32, (toks, toks), 0) + lax.broadcasted_iota(jnp.int32, (toks, toks), 1)
        == toks - 1
    )
    hid[...] = flip.astype(bf16)
    doff[...] = jnp.zeros(doff.shape, f32)

    def attend_back(h, carry):
        head = pl.ds(pl.multiple_of(h * hs, hs), hs)
        grad_v = []
        grad_k = []
        offsets = jnp.zeros((1, lanes), f32)
        for block in (0, 1):
            p, low, keys = softmax_block(h, head, block)
            q_rows = qt[head, low : low + half_tok]
            a_rows = dat[head, low : low + half_tok]
            grad_p = dot_tn(a_rows, vt[head, 0:keys])
            ds = (p * (grad_p - jnp.sum(p * grad_p, axis=1, keepdims=True))).astype(bf16)
            grad_v.append(dot_nn(a_rows, p.astype(bf16)))
            grad_k.append(dot_nn(q_rows, ds))
            dqt[head, low : low + half_tok] = dot_nt(kt[head, 0:keys], ds).astype(bf16)
            turned = dot_nn(ds, hid[0:keys, toks - keys : toks])
            padded = jnp.concatenate([turned, jnp.zeros((half_tok, lanes - keys), f32)], axis=1)
            lined = pltpu.roll(padded, half_tok, 1, stride=1, stride_axis=0)
            offsets = offsets + jnp.sum(lined, axis=0, keepdims=True)
        for dst, parts in ((dvt, grad_v), (dkt, grad_k)):
            dst[head, 0:half_tok] = (parts[0] + parts[1][:, 0:half_tok]).astype(bf16)
            dst[head, half_tok:toks] = parts[1][:, half_tok:toks].astype(bf16)
        doff[pl.ds(h, 1), :] = offsets
        return carry

    lax.fori_loop(0, heads // 2, attend_back, 0)
    rep_turn(nv - 2, fw)
    rep_send(nv - 1, fw)
    lax.fori_loop(heads // 2, heads, attend_back, 0)
    rep_last(nv - 2, fw)
    rep_turn(nv - 1, fw)
    weight_grad(nv, 0, n1t, dvt)
    core_send(nv, aw)
    weight_grad(nq, 0, n1t, dqt)
    weight_grad(nq, 1, n1t, dkt)
    plane_send(nv, aw)
    core_send(nq, aw)
    rep_last(nv - 1, fw)
    plane_send(nq, aw)

    def first_back(i, acc):
        sl = pl.ds(pl.multiple_of(i * big, 16), big)
        gn = dot_nn(wq[sl, :], dqt[...]) + dot_nn(wk[sl, :], dkt[...]) + dot_nn(wv[sl, :], dvt[...])
        acc_o[sl, :] = gn
        v = gcol[sl, 0:1] * gn * xt_ref[sl, :].astype(f32)
        return acc + jnp.sum(v.reshape(big // 8, 8, toks), axis=0)

    back = jnp.sum(lax.fori_loop(0, nbig, first_back, zero8), axis=0, keepdims=True) * (1.0 / width)
    back = back * (r1 * r1 * r1)
    plane_turn(nv, aw)

    def first_norm(sl, carry):
        v = xt_ref[sl, :].astype(f32)
        gn = acc_o[sl, :]
        prod = gn * v * r1
        hi = prod.astype(bf16)
        wg2[sl, :] = hi
        wu2[sl, :] = (prod - hi.astype(f32)).astype(bf16)
        gtok_ref[sl, :] = (acc_n[sl, :] + r1 * gcol[sl, 0:1] * gn - v * back).astype(bf16)
        return carry

    over_rows(first_norm, 0)
    sms[0, :, 0:width] += token_sums(0)
    rest = doff[...]
    table = jnp.zeros((8, onehot.shape[0]), f32)
    for _ in range(3):
        part = rest.astype(bf16)
        table = table + dot_nt(part, onehot[...])
        rest = rest - part.astype(f32)
    sms[0, :, sms.shape[2] - onehot.shape[0] : sms.shape[2]] = table
    small_send(0)
    plane_turn(nq, aw)
    small_step(0)
    rep_send(nv, aw)
    small_step(1)
    rep_send(nq, aw)
    small_step(2)
    rep_turn(nv, aw)
    small_step(3)
    rep_last(nv, aw)
    rep_turn(nq, aw)
    small_step(4)
    rep_last(nq, aw)
    small_step(5)

    settle(gland.at[pl.ds(0, 7)], gain_s)
    lax.fori_loop(0, chunks, lambda k, carry: (gather_sent(("f", k)), carry)[1], 0)

    @pl.when(outer)
    def _():
        for n in (nv, nq):
            settle(span(vbuf, (n % 2) * 2, 2, aw), zis.at[n])
        for n in range(total):
            for half in (0, 1):
                settle(cut1(ubuf, 0, width_of(n)), ur.at[n, half])

    @pl.when(inner)
    def _():
        for n in (nv, nq):
            u_free(n, aw)
        for n in range(total):
            settle(cut1(ubuf, 0, width_of(n)), ur.at[n, 1 - c])


def fused(tokens, cotangent, buckets, bias_table, gains, weights):
    toks, width = tokens.shape
    heads = bias_table.shape[1]
    rows, aw = weights[0].shape
    ff = weights[4].shape[1]
    sub = 256
    fw = 3 * sub
    chunks = ff // (2 * sub)
    total = chunks + 2
    lanes = 2 * toks
    small_lanes = (width + 127) // 128 * 128 + 128
    padded = jnp.concatenate([buckets, jnp.full((1,), -1, jnp.int32)])
    turned = jnp.concatenate([buckets[::-1], jnp.full((1,), -1, jnp.int32)])
    bucket_rows = jnp.concatenate([turned[None], padded[None], jnp.full((6, lanes), -1, jnp.int32)])
    table = jnp.pad(bias_table.T, ((0, 8 - heads), (0, 128 - bias_table.shape[0])))
    vm = pl.BlockSpec(memory_space=pltpu.VMEM)
    hbm = pl.BlockSpec(memory_space=pltpu.HBM)
    dma = pltpu.SemaphoreType.DMA
    tok = lambda kind: pltpu.VMEM((width, toks), kind)
    inner_rows = pltpu.VMEM((aw, toks), bf16)
    blocks = lambda count: pltpu.VMEM((count, rows, fw), bf16)
    return pl.pallas_call(
        functools.partial(fused_kernel, chunks=chunks, heads=heads),
        out_shape=(
            jax.ShapeDtypeStruct((width, toks), bf16),
            jax.ShapeDtypeStruct((width, toks), bf16),
            jax.ShapeDtypeStruct((8, small_lanes), f32),
            *([jax.ShapeDtypeStruct((rows, aw), bf16)] * 4),
            *([jax.ShapeDtypeStruct((rows, ff), bf16)] * 3),
            jax.ShapeDtypeStruct((chunks, 16, rows, fw), bf16),
        ),
        in_specs=[vm] * 5 + [hbm] * 7,
        out_specs=[vm] * 3 + [hbm] * 8,
        scratch_shapes=[
            pltpu.VMEM((8, rows, 128), bf16),
            pltpu.VMEM((width, 128), f32),
            tok(bf16),
            tok(bf16),
            tok(f32),
            tok(f32),
            tok(f32),
            *([inner_rows] * 8),
            *([pltpu.VMEM((width, aw), bf16)] * 4),
            *([pltpu.VMEM((width, 2 * sub), bf16)] * 3),
            pltpu.VMEM((16, rows, sub), bf16),
            blocks(32),
            *([pltpu.VMEM((toks, 2 * sub), bf16)] * 3),
            blocks(16),
            blocks(8),
            *([blocks(4)] * 5),
            pltpu.VMEM((8, lanes), f32),
            pltpu.VMEM((128, lanes), bf16),
            pltpu.VMEM((8, lanes), f32),
            pltpu.VMEM((6, 8, small_lanes), f32),
            pltpu.VMEM((6, 8, small_lanes), f32),
            dma(()),
            dma(()),
            *([dma((total,))] * 5),
            dma((2,)),
            *([dma((total,))] * 10),
            dma((total, 3)),
            dma((total,)),
            dma((total, 2)),
            dma((6,)),
            dma((6,)),
            pltpu.SemaphoreType.REGULAR,
        ],
        compiler_params=pltpu.CompilerParams(
            collective_id=0, has_side_effects=True, vmem_limit_bytes=60 * 2**20
        ),
        cost_estimate=pl.CostEstimate(flops=57 * 10**9, bytes_accessed=10**8, transcendentals=10**7),
    )(tokens.T, cotangent.T, bucket_rows, table, gains, *weights)


def fused_body(
    tokens,
    cotangent,
    buckets,
    bias_table,
    attn_gain,
    w_query,
    w_key,
    w_value,
    w_output,
    ffn_gain,
    w_gate,
    w_up,
    w_down,
):
    rows = w_query.shape[0]
    gains = jnp.pad(jnp.stack([attn_gain, ffn_gain], axis=1), ((0, 0), (0, 126)))
    weights = (w_query, w_key, w_value, w_output, w_gate, w_up, w_down)
    out, gtok, small, *grads = fused(tokens, cotangent, buckets, bias_table, gains, weights)
    grads = [grad.astype(f32) for grad in grads[:7]]
    own = lax.dynamic_slice(small, (0, lax.axis_index("shard") * rows), (2, rows))
    table = small[0 : bias_table.shape[1], small.shape[1] - 128 :][:, 0 : bias_table.shape[0]].T
    return (out.T, gtok.T, own[0], *grads[:4], own[1], *grads[4:], table)


def solution(mesh):
    chosen = body
    if mesh.shape["shard"] == 8 and mesh.shape["rep"] == 4:
        chosen = fused_body
    return jax.shard_map(
        chosen,
        mesh=mesh,
        in_specs=(
            P(("shard", "rep"), None),
            P(("shard", "rep"), None),
            P(),
            P(),
            P("shard"),
            P("shard", None),
            P("shard", None),
            P("shard", None),
            P("shard", None),
            P("shard"),
            P("shard", None),
            P("shard", None),
            P("shard", None),
        ),
        out_specs=(
            P(("shard", "rep"), None),
            P(("shard", "rep"), None),
            P("shard"),
            P("shard", None),
            P("shard", None),
            P("shard", None),
            P("shard", None),
            P("shard"),
            P("shard", None),
            P("shard", None),
            P("shard", None),
            P(),
        ),
        check_vma=False,
    )
```

profile of v0, /device:TPU:1, one launch (start us, length us, event | category | flops | bytes accessed | tf_op | source)
XLA Modules:
  0.0 387.5 jit_solution(17682472745067475704)
XLA Ops:
  0.6 0.8 reverse
  1.4 0.1 slice.15
  1.5 0.8 pad_add_fusion
  2.2 0.1 pad.14.clone
  2.3 0.7 add_add_fusion.buckets_ref
  3.0 0.7 stack.10
  3.7 0.7 stack.9
  4.3 0.1 copy.27
  4.5 0.6 pad.9.gains_ref
  5.1 1.3 pad.8.table_ref
  6.4 365.6 %shard_map.220 = (bf16[1472,512]{1,0:T(8,128)(2,1)}, bf16[1472,512]{1,0:T(8,128)(2,1)}, f32[8,1664]{1,0:T(8,128)}, bf16[184,384]{1,0:T(8,128)(2,1)}, bf16[184,38...) custom-call(bf16[1472,512]{1,0:T(8,128)(2,1)} %bitcast.20, ...), custom_call_target="tpu_custom_call" | custom-call | flops 57000001536 | bytes 100000000 | tf_op jit(solution)/shard_map/pallas_call | solution.py:1095
  372.0 1.4 fusion
  373.4 1.3 slice_bitcast_fusion
  374.7 0.0 copy-start.3
  374.7 3.2 convert_element_type.29
  377.9 0.0 copy-done.3
  377.9 0.0 copy-start.2
  377.9 1.8 convert_element_type.30
  379.7 0.0 copy-done.2
  379.7 0.0 copy-start.7
  379.7 0.0 copy-start.6
  379.7 0.0 copy-start.5
  379.7 0.0 copy-start.4
  379.8 1.8 convert_element_type.31
  381.5 0.0 copy-start.1
  381.6 0.0 copy-done.7
  381.6 0.7 convert_element_type.25
  382.3 0.0 copy-done.6
  382.3 0.7 convert_element_type.26
  383.0 0.0 copy-done.5
  383.0 0.7 convert_element_type.27
  383.7 0.0 copy-done.4
  383.8 0.7 convert_element_type.28
  384.5 0.0 copy-done.1
  384.5 0.0 copy-start
  384.5 1.1 copy.30
  385.6 0.8 copy-done
  386.4 1.1 copy.31
  (2 shorter events, 0.0 us)
Async XLA Ops:
  374.7 3.2 copy-start.3
  377.9 1.8 copy-start.2
  379.7 1.8 copy-start.7
  379.7 2.5 copy-start.6
  379.7 3.3 copy-start.5
  379.7 4.0 %copy-start.4 = (bf16[184,384]{1,0:T(8,128)(2,1)S(1)}, bf16[184,384]{1,0:T(8,128)(2,1)}, u32[]{:S(2)}) copy-start(bf16[184,384]{1,0:T(8,128)(2,1)} %get-tuple-element.28) | copy-start | bytes 423940
  381.5 2.9 copy-start.1
  384.5 1.9 copy-start
where the time goes:
time: 388 us
  Pallas kernels  366 us (94%)
  other arithmetic  11.2 us (3%)
  local copies, waits for them, and re-layouts  10.1 us (3%)
    pallas_call x1, Pallas kernels, fused(): pl.pallas_call(functools.partial(fused_kernel, chunks=chunks, heads=heads...  366 us
    convert_element_type x7, other arithmetic, fused_body(): grads = [grad.astype(f32) for grad in grads[:7]]  9.72 us

commit v1 on v0

--- a/solution.py
+++ b/solution.py
@@ -272,6 +272,21 @@
         small_total[2],
     )
 
+HEAD_SLOTS = 7
+TAIL_SLOTS = 12
+HELPED = (1, 2, 4, 5)
+SLOTS = {
+    "send": (0, 0, 1, 2, 2, 4, 6),
+    "forward": (1, 1, 5, 7, 8, 10, 16),
+    "swap": (2, 3, 7, 10, 11, 12, 18),
+    "get_forward": (2, 6, 11, 12, 14, 15, 18),
+    "get_swap": (5, 6, 11, 12, 14, 16, 19),
+    "turn": (10, 12, 15, 16, 18, 20, 23, 26, 28),
+    "rep": (13, 15, 16, 18, 21, 22, 24, 28, 30),
+    "mid": (15, 16, 18, 20, 22, 24, 25, 30, 31),
+    "last": (16, 18, 20, 22, 24, 25, 28, 31, 32),
+}
+
 
 def dot_nn(a, b):
     return lax.dot_general(a, b, (((1,), (0,)), ((), ())), preferred_element_type=f32)
@@ -309,6 +324,9 @@
     gu_ref,
     gd_ref,
     land_ref,
+    sum_ref,
+    hop_ref,
+    turn_ref,
     gland,
     gcol,
     n1t,
@@ -337,8 +355,8 @@
     dgt,
     dup,
     rc,
-    rxy,
-    r2,
+    stage_t,
+    stage_v,
     vbuf,
     zi,
     zm,
@@ -358,6 +376,8 @@
     load_sem,
     e0s,
     e0r,
+    sum_sem,
+    stage_sem,
     e1s,
     e1r,
     e2s,
@@ -379,7 +399,7 @@
     width = xt_ref.shape[0]
     toks = xt_ref.shape[1]
     rows = gains_ref.shape[0]
-    fw = land_ref.shape[3]
+    fw = land_ref.shape[2]
     sub = fw // 3
     aw = wq_ref.shape[1]
     hs = aw // heads
@@ -434,13 +454,30 @@
         kind, k = chunk
         if kind == "a":
             return g.at[16 + index, :, pl.ds(k * aw, aw)]
-        return land_ref.at[k, index]
+        return land_ref.at[k * 16 + index]
 
     def places(chunk, count):
         kind, k = chunk
         if kind == "a":
             return g.at[pl.ds(16, count), :, pl.ds(k * aw, aw)]
-        return land_ref.at[k, pl.ds(0, count)]
+        return land_ref.at[pl.ds(0, count)]
+
+    def any_of(value, options):
+        return functools.reduce(jnp.logical_or, [value == option for option in options], jnp.bool_(False))
+
+    def helped(chunk):
+        kind, k = chunk
+        return False if kind == "a" else any_of(k, HELPED)
+
+    def active(chunk):
+        kind, k = chunk
+        return True if kind == "a" else jnp.logical_not(any_of(k, HELPED)) | (r % 2 == k % 2)
+
+    def when(condition, then):
+        if condition is True:
+            then()
+        elif condition is not False:
+            pl.when(condition)(then)
 
     def columns(k, half):
         return pl.ds(pl.multiple_of((2 * k + half) * sub, sub), sub)
@@ -460,32 +497,49 @@
 
     def gather_send(chunk):
         i = at(chunk)
-        for half in (0, 1):
-            for src, dst in own_parts(chunk, half):
-                remote(src, dst, gsend.at[i], g1r.at[i], (bx + half, r)).start()
-                remote(src, dst, gsend.at[i], g1r.at[i], (by + half, r)).start()
+
+        def cross():
+            for half in (0, 1):
+                for src, dst in own_parts(chunk, half):
+                    remote(src, dst, gsend.at[i], g1r.at[i], (bx + half, r)).start()
+                    remote(src, dst, gsend.at[i], g1r.at[i], (by + half, r)).start()
+
+        when(active(chunk), cross)
         for half in (0, 1):
             for src, dst in own_parts(chunk, half):
                 remote(src, dst, gsend.at[i], gpr.at[i], (sc, r)).start()
                 pltpu.make_async_copy(src, dst, gloc.at[i]).start()
 
+    def hand_over(chunk, blocks, sem):
+        i = at(chunk)
+
+        def hand():
+            for b in blocks:
+                spot = place(chunk, c * 8 + b)
+                remote(spot, spot, gsend.at[i], sem.at[i], (s, mate)).start()
+
+        if chunk[0] == "f":
+            pl.when(helped(chunk) & active(chunk))(hand)
+        for b in blocks:
+            spot = place(chunk, c * 8 + b)
+            remote(spot, spot, gsend.at[i], gpr.at[i], (sc, r)).start()
+
     def gather_forward(chunk):
         i = at(chunk)
         settle(places(chunk, 4), g1r.at[i])
-        one = place(chunk, c * 8 + bx)
-        two = place(chunk, c * 8 + by + 1)
-        remote(one, one, gsend.at[i], g2r.at[i], (sy, r)).start()
-        remote(two, two, gsend.at[i], g2r.at[i], (sx, r)).start()
-        for b in (bx, bx + 1, by, by + 1):
-            spot = place(chunk, c * 8 + b)
-            remote(spot, spot, gsend.at[i], gpr.at[i], (sc, r)).start()
+
+        def cross():
+            one = place(chunk, c * 8 + bx)
+            two = place(chunk, c * 8 + by + 1)
+            remote(one, one, gsend.at[i], g2r.at[i], (sy, r)).start()
+            remote(two, two, gsend.at[i], g2r.at[i], (sx, r)).start()
+
+        when(active(chunk), cross)
+        hand_over(chunk, (bx, bx + 1, by, by + 1), g1r)
 
     def gather_swap(chunk):
-        i = at(chunk)
-        settle(places(chunk, 2), g2r.at[i])
-        for b in (bd, bd + 1):
-            spot = place(chunk, c * 8 + b)
-            remote(spot, spot, gsend.at[i], gpr.at[i], (sc, r)).start()
+        settle(places(chunk, 2), g2r.at[at(chunk)])
+        hand_over(chunk, (bd, bd + 1), g2r)
 
     def gather_done(chunk):
         i = at(chunk)
@@ -493,7 +547,19 @@
         settle(places(chunk, 2), gloc.at[i])
 
     def gather_sent(chunk):
-        settle(places(chunk, 14), gsend.at[at(chunk)])
+        i = at(chunk)
+        does = active(chunk)
+        if does is True:
+            settle(places(chunk, 14), gsend.at[i])
+            return
+        pl.when(does & helped(chunk))(lambda: settle(places(chunk, 20), gsend.at[i]))
+        pl.when(does & jnp.logical_not(helped(chunk)))(lambda: settle(places(chunk, 14), gsend.at[i]))
+        pl.when(jnp.logical_not(does))(lambda: settle(places(chunk, 8), gsend.at[i]))
+
+    def ahead(stage, k, mine):
+        chunk = ("f", k)
+        does = active(chunk) if mine else jnp.logical_not(active(chunk))
+        pl.when((k < chunks) & does)(lambda: stage(chunk))
 
     def cut(ref, w):
         return ref if w == fw else ref.at[:, :, pl.ds(0, w)]
@@ -517,58 +583,98 @@
         value = get(dst, i, w).astype(f32) + get(src, j, w).astype(f32)
         put(dst, i, w, value.astype(bf16))
 
-    def core_send(n, w):
+    def core_part(n, b, count, w):
         slot = n % 2
         remote(
-            span(g, slot * 16 + (1 - c) * 8, 8, w), span(rc, slot * 8, 8, w), e0s.at[n], e0r.at[n], (sc, r)
+            span(g, slot * 16 + (1 - c) * 8 + b, count, w), span(rc, slot * 8 + b, count, w), e0s.at[n], e0r.at[n], (sc, r)
         ).start()
 
     def plane_send(n, w):
         slot = n % 2
         base = slot * 16 + c * 8
         settle(span(rc, slot * 8, 8, w), e0r.at[n])
-
-        @pl.loop(0, 8)
-        def _(b):
+        order = []
+        for k, kx, ky in ((0, 1 - y, 1 - x), (1, y, x)):
+            order.append((4 * kx + 2 * (1 - x), sx, 2 * k))
+            order.append((4 * (1 - y) + 2 * ky + 1, sy, 2 * k + 1))
+        order += [(b, None, None) for b in (4 * (1 - y) + 2 * x, 4 * y + 2 * (1 - x) + 1, b_own, b_own + 1)]
+
+        def store(i):
+            b = order[i][0]
+            return pltpu.make_async_copy(cut1(g, base + b, w), cut1(sum_ref, n * 8 + b, w), sum_sem.at[i])
+
+        for i, (b, _, _) in enumerate(order):
             add_to(g, base + b, rc, slot * 8 + b, w)
-
-        for k in (0, 1):
-            remote(
-                cut1(g, base + 4 * k + 2 * (1 - x), w), cut1(rxy, slot * 4 + k, w), e1s.at[n], e1r.at[n], (sx, r)
-            ).start()
-            remote(
-                cut1(g, base + 4 * (1 - y) + 2 * k + 1, w),
-                cut1(rxy, slot * 4 + 2 + k, w),
-                e1s.at[n],
-                e1r.at[n],
-                (sy, r),
-            ).start()
-
-    def plane_turn(n, w):
+            store(i).start()
+        for i, (b, dev, spot) in enumerate(order):
+            store(i).wait()
+            if dev is not None:
+                remote(
+                    cut1(sum_ref, n * 8 + b, w), cut1(hop_ref, n * 4 + spot, w), e1s.at[n], e1r.at[n, spot // 2], (dev, r)
+                ).start()
+
+    def slot_free(n):
+        settle(span(g, 0, 8, width_of(n)), e0s.at[n])
+
+    def turn_free(n):
+        settle(span(turn_ref, 0, 2, width_of(n)), e2s.at[n])
+
+    def guarded(n, least, then):
+        if isinstance(n, int):
+            if n >= least:
+                then()
+        else:
+            pl.when(n >= least)(then)
+
+    def turn_loads(n, w):
+        base = (n % 2) * 4
+        first = n * 8 + 4 * (1 - y) + 2 * x
+        second = n * 8 + 4 * y + 2 * (1 - x) + 1
+        return [
+            pltpu.make_async_copy(cut1(sum_ref, first, w), cut1(stage_t, base, w), stage_sem.at[0]),
+            pltpu.make_async_copy(cut1(sum_ref, second, w), cut1(stage_t, base + 1, w), stage_sem.at[1]),
+            pltpu.make_async_copy(span(hop_ref, n * 4, 2, w), span(stage_t, base + 2, 2, w), stage_sem.at[2]),
+        ]
+
+    def turn_start(n, w):
+        guarded(n, 2, lambda: turn_free(n - 2))
+        settle(span(hop_ref, 0, 2, w), e1r.at[n, 0])
+        for load in turn_loads(n, w):
+            load.start()
+
+    def turn_end(n, w):
+        base = (n % 2) * 4
+        for load in turn_loads(n, w):
+            load.wait()
+        for j, dev in ((0, sy), (1, sx)):
+            add_to(stage_t, base + j, stage_t, base + 2 + j, w)
+            remote(cut1(stage_t, base + j, w), cut1(turn_ref, n * 2 + j, w), e2s.at[n], e2r.at[n], (dev, r)).start()
+
+    def rep_loads(n, w):
+        return [
+            pltpu.make_async_copy(span(sum_ref, n * 8 + b_own, 2, w), span(stage_v, 0, 2, w), stage_sem.at[3]),
+            pltpu.make_async_copy(span(hop_ref, n * 4 + 2, 2, w), span(stage_v, 2, 2, w), stage_sem.at[4]),
+            pltpu.make_async_copy(span(turn_ref, n * 2, 2, w), span(stage_v, 4, 2, w), stage_sem.at[5]),
+        ]
+
+    def rep_start(n, w):
+        settle(span(hop_ref, 0, 2, w), e1r.at[n, 1])
+        settle(span(turn_ref, 0, 2, w), e2r.at[n])
+        for load in rep_loads(n, w):
+            load.start()
+
+    def rep_end(n, w):
         slot = n % 2
-        base = slot * 16 + c * 8
-        settle(span(rxy, slot * 4, 4, w), e1r.at[n])
-        first = base + 4 * (1 - y) + 2 * x
-        second = base + 4 * y + 2 * (1 - x) + 1
-        mine = base + b_own
-        add_to(g, first, rxy, slot * 4 + 1 - y, w)
-        add_to(g, second, rxy, slot * 4 + 2 + 1 - x, w)
-        add_to(g, mine, rxy, slot * 4 + y, w)
-        add_to(g, mine + 1, rxy, slot * 4 + 2 + x, w)
-        remote(cut1(g, first, w), cut1(r2, slot * 2, w), e2s.at[n], e2r.at[n], (sy, r)).start()
-        remote(cut1(g, second, w), cut1(r2, slot * 2 + 1, w), e2s.at[n], e2r.at[n], (sx, r)).start()
-
-    def rep_send(n, w):
-        slot = n % 2
-        base = slot * 16 + c * 8
-        settle(span(r2, slot * 2, 2, w), e2r.at[n])
         if isinstance(n, int):
             if n >= 2:
                 pl.when(outer)(functools.partial(rep_free, n))
         else:
             pl.when(outer & (n >= 2))(functools.partial(rep_free, n))
+        for load in rep_loads(n, w):
+            load.wait()
         for j in (0, 1):
-            value = get(g, base + b_own + j, w).astype(f32) + get(r2, slot * 2 + j, w).astype(f32)
+            value = get(stage_v, j, w).astype(f32) + get(stage_v, 2 + j, w).astype(f32)
+            value = value + get(stage_v, 4 + j, w).astype(f32)
             put(vbuf, slot * 2 + j, w, value.astype(bf16))
 
         @pl.when(outer)
@@ -576,10 +682,6 @@
             remote(
                 span(vbuf, slot * 2, 2, w), span(zi, slot * 2, 2, w), zis.at[n], zir.at[n], (s, mate)
             ).start()
-
-        settle(span(g, slot * 16, 8, w), e0s.at[n])
-        settle(span(rxy, slot * 4, 4, w), e1s.at[n])
-        settle(span(r2, slot * 2, 2, w), e2s.at[n])
 
     def width_of(n):
         return fw if not isinstance(n, int) or n < chunks else aw
@@ -657,6 +759,45 @@
                 pl.when(c == 1)(lambda: finish(1))
             settle(span(vbuf, slot * 2, 2, w), zms.at[n])
 
+    def gathers(stage, mine):
+        return lambda k: ahead(stage, k, mine)
+
+    def reduces(stage):
+        return lambda n: stage(n, width_of(n))
+
+    order = (
+        ("swap", gathers(gather_swap, True)),
+        ("forward", gathers(gather_forward, True)),
+        ("send", lambda k: gather_send(("f", k))),
+        ("turn", reduces(turn_start)),
+        ("last", reduces(rep_last)),
+        ("mid", reduces(rep_turn)),
+        ("turn", reduces(turn_end)),
+        ("rep", reduces(rep_start)),
+        ("get_forward", gathers(gather_forward, False)),
+        ("get_swap", gathers(gather_swap, False)),
+        ("rep", reduces(rep_end)),
+    )
+    loop_at = HEAD_SLOTS
+    tail_at = HEAD_SLOTS + 2 * chunks
+
+    def do(slot):
+        for name, stage in order:
+            for n, spot in enumerate(SLOTS[name]):
+                if spot == slot:
+                    stage(n)
+
+    def do_in_loop(t, side):
+        for name, stage in order:
+            pairs = [
+                ((spot - loop_at) // 2, n)
+                for n, spot in enumerate(SLOTS[name])
+                if loop_at <= spot < tail_at and (spot - loop_at) % 2 == side
+            ]
+            if pairs:
+                n = sum([jnp.where(t == step, number, 0) for step, number in pairs], jnp.int32(0))
+                pl.when(any_of(t, [step for step, _ in pairs]))(functools.partial(stage, n))
+
     def small_send(step):
         if step < 3:
             dev = ((sc, r), (sx, r), (sy, r))[step]
@@ -742,7 +883,7 @@
         remote(gains_ref, gdst, gain_s, gain_r, dev).start()
     pltpu.make_async_copy(gains_ref, gdst, load_sem.at[1]).start()
     gather_send(("a", 1))
-    gather_send(("f", 0))
+    do(0)
 
     def square_sum(sl, acc):
         v = xt_ref[sl, :].astype(f32)
@@ -767,10 +908,11 @@
         return carry
 
     gather_forward(("a", 0))
+    do(1)
     over_rows(norm_one, 0)
     gather_swap(("a", 0))
     gather_forward(("a", 1))
-    gather_send(("f", 1))
+    do(2)
 
     def compact(dst, half, col):
         @pl.loop(0, nbig)
@@ -790,12 +932,12 @@
     compact(wk, 1, 0)
     kt[...] = dot_tn(wk[...], n1t[...]).astype(bf16)
     gather_swap(("a", 1))
+    do(3)
     gather_done(("a", 1))
     compact(wv, 0, aw)
     vt[...] = dot_tn(wv[...], n1t[...]).astype(bf16)
     compact(wo, 1, aw)
-    gather_forward(("f", 0))
-    gather_send(("f", 2))
+    do(4)
 
     half_tok = toks // 2
 
@@ -816,9 +958,9 @@
         return carry
 
     lax.fori_loop(0, heads // 2, attend, 0)
-    gather_swap(("f", 0))
-    gather_forward(("f", 1))
+    do(5)
     lax.fori_loop(heads // 2, heads, attend, 0)
+    do(6)
 
     def branch_one(i, acc):
         sl = pl.ds(pl.multiple_of(i * big, 16), big)
@@ -847,7 +989,7 @@
         def load(p):
             half, k = parts[p]
             return pltpu.make_async_copy(
-                land_ref.at[t, pl.ds(half * 8, 8), :, pl.ds(k * sub, sub)],
+                land_ref.at[pl.ds(t * 16 + half * 8, 8), :, pl.ds(k * sub, sub)],
                 wload.at[pl.ds((p % 2) * 8, 8)],
                 load_sem.at[p % 2],
             )
@@ -896,18 +1038,14 @@
                         g[slot * 16 + half * 8 + 2 * i + j, :, k * sub : (k + 1) * sub] = value[
                             rows * j : rows * (j + 1), half * sub : (half + 1) * sub
                         ].astype(bf16)
+            core_part(t, 2 * i, 2, fw)
 
     def ffn_step(t, carry):
-        pl.when(t + 1 < chunks)(lambda: gather_swap(("f", t + 1)))
-        pl.when(t + 2 < chunks)(lambda: gather_forward(("f", t + 2)))
-        pl.when(t + 3 < chunks)(lambda: gather_send(("f", t + 3)))
-        pl.when(t >= 3)(lambda: rep_turn(t - 3, fw))
-        pl.when(t >= 2)(lambda: rep_send(t - 2, fw))
+        do_in_loop(t, 0)
+        pl.when(t >= 2)(lambda: slot_free(t - 2))
         gather_done(("f", t))
         ffn_chunk(t)
-        core_send(t, fw)
-        pl.when(t >= 3)(lambda: rep_last(t - 3, fw))
-        pl.when(t >= 1)(lambda: plane_turn(t - 1, fw))
+        do_in_loop(t, 1)
         plane_send(t, fw)
         return carry
 
@@ -917,8 +1055,7 @@
 
     nv = chunks
     nq = chunks + 1
-    rep_turn(nv - 3, fw)
-    rep_send(nv - 2, fw)
+    do(tail_at)
     pick = lax.broadcasted_iota(jnp.int32, (8, toks), 0)
 
     def token_sums(row):
@@ -947,8 +1084,7 @@
     over_rows(second_norm, 0)
     sms[0] = jnp.zeros(sms.shape[1:], f32)
     sms[0, :, 0:width] = token_sums(1)
-    rep_last(nv - 3, fw)
-    plane_turn(nv - 1, fw)
+    do(tail_at + 1)
 
     dat[...] = dot_tn(wo[...], n2t[...]).astype(bf16)
 
@@ -960,7 +1096,9 @@
             for j in (0, 1):
                 g[(n % 2) * 16 + half * 8 + 2 * i + j, :, 0:aw] = value[rows * j : rows * (j + 1), :].astype(bf16)
 
+    slot_free(5)
     weight_grad(nv, 1, n2t, att)
+    do(tail_at + 2)
     flip = (
         lax.broadcasted_iota(jnp.int32, (toks, toks), 0) + lax.broadcasted_iota(jnp.int32, (toks, toks), 1)
         == toks - 1
@@ -993,19 +1131,18 @@
         return carry
 
     lax.fori_loop(0, heads // 2, attend_back, 0)
-    rep_turn(nv - 2, fw)
-    rep_send(nv - 1, fw)
+    do(tail_at + 3)
     lax.fori_loop(heads // 2, heads, attend_back, 0)
-    rep_last(nv - 2, fw)
-    rep_turn(nv - 1, fw)
     weight_grad(nv, 0, n1t, dvt)
-    core_send(nv, aw)
+    core_part(nv, 0, 8, aw)
+    slot_free(6)
     weight_grad(nq, 0, n1t, dqt)
     weight_grad(nq, 1, n1t, dkt)
     plane_send(nv, aw)
-    core_send(nq, aw)
-    rep_last(nv - 1, fw)
+    core_part(nq, 0, 8, aw)
+    do(tail_at + 4)
     plane_send(nq, aw)
+    do(tail_at + 5)
 
     def first_back(i, acc):
         sl = pl.ds(pl.multiple_of(i * big, 16), big)
@@ -1016,7 +1153,7 @@
 
     back = jnp.sum(lax.fori_loop(0, nbig, first_back, zero8), axis=0, keepdims=True) * (1.0 / width)
     back = back * (r1 * r1 * r1)
-    plane_turn(nv, aw)
+    do(tail_at + 6)
 
     def first_norm(sl, carry):
         v = xt_ref[sl, :].astype(f32)
@@ -1038,21 +1175,18 @@
         rest = rest - part.astype(f32)
     sms[0, :, sms.shape[2] - onehot.shape[0] : sms.shape[2]] = table
     small_send(0)
-    plane_turn(nq, aw)
-    small_step(0)
-    rep_send(nv, aw)
-    small_step(1)
-    rep_send(nq, aw)
-    small_step(2)
-    rep_turn(nv, aw)
-    small_step(3)
-    rep_last(nv, aw)
-    rep_turn(nq, aw)
-    small_step(4)
-    rep_last(nq, aw)
-    small_step(5)
+    for k in range(7, TAIL_SLOTS):
+        do(tail_at + k)
+        for step in {7: (0,), 8: (1,), 9: (2, 3), 10: (4, 5)}.get(k, ()):
+            small_step(step)
 
     settle(gland.at[pl.ds(0, 7)], gain_s)
+    slot_free(nv)
+    slot_free(nq)
+    turn_free(nv)
+    turn_free(nq)
+    for n in range(total):
+        settle(span(hop_ref, 0, 4, width_of(n)), e1s.at[n])
     lax.fori_loop(0, chunks, lambda k, carry: (gather_sent(("f", k)), carry)[1], 0)
 
     @pl.when(outer)
@@ -1100,10 +1234,13 @@
             jax.ShapeDtypeStruct((8, small_lanes), f32),
             *([jax.ShapeDtypeStruct((rows, aw), bf16)] * 4),
             *([jax.ShapeDtypeStruct((rows, ff), bf16)] * 3),
-            jax.ShapeDtypeStruct((chunks, 16, rows, fw), bf16),
+            jax.ShapeDtypeStruct((chunks * 16, rows, fw), bf16),
+            jax.ShapeDtypeStruct((total * 8, rows, fw), bf16),
+            jax.ShapeDtypeStruct((total * 4, rows, fw), bf16),
+            jax.ShapeDtypeStruct((total * 2, rows, fw), bf16),
         ),
         in_specs=[vm] * 5 + [hbm] * 7,
-        out_specs=[vm] * 3 + [hbm] * 8,
+        out_specs=[vm] * 3 + [hbm] * 11,
         scratch_shapes=[
             pltpu.VMEM((8, rows, 128), bf16),
             pltpu.VMEM((width, 128), f32),
@@ -1120,7 +1257,8 @@
             *([pltpu.VMEM((toks, 2 * sub), bf16)] * 3),
             blocks(16),
             blocks(8),
-            *([blocks(4)] * 5),
+            blocks(6),
+            *([blocks(4)] * 4),
             pltpu.VMEM((8, lanes), f32),
             pltpu.VMEM((128, lanes), bf16),
             pltpu.VMEM((8, lanes), f32),
@@ -1130,7 +1268,12 @@
             dma(()),
             *([dma((total,))] * 5),
             dma((2,)),
-            *([dma((total,))] * 10),
+            *([dma((total,))] * 2),
+            dma((8,)),
+            dma((6,)),
+            dma((total,)),
+            dma((total, 2)),
+            *([dma((total,))] * 6),
             dma((total, 3)),
             dma((total,)),
             dma((total, 2)),

time: 388 us -> 335 us (0.86)
  Pallas kernels: 366 us -> 311 us
    pallas_call x1, Pallas kernels: 366 us -> 311 us  [fused(): pl.pallas_call(functools.partial(fused_kernel, chunks=chunks, heads=heads...]
where the time goes in v1:
time: 335 us; the launch traced here: 333 us
  Pallas kernels  311 us (93%)
  other arithmetic  11.2 us (3%)
  local copies, waits for them, and re-layouts  10.1 us (3%)
    pallas_call x1, Pallas kernels, fused(): pl.pallas_call(functools.partial(fused_kernel, chunks=chunks, heads=heads...  311 us
    convert_element_type x7, other arithmetic, fused_body(): grads = [grad.astype(f32) for grad in grads[:7]]  9.72 us

profile of v1, /device:TPU:1, one launch (start us, length us, event | category | flops | bytes accessed | tf_op | source)
XLA Modules:
  0.0 333.3 jit_solution(17360470735904252960)
XLA Ops:
  0.6 0.8 reverse
  1.4 0.1 slice.15
  1.5 0.8 pad_add_fusion
  2.2 0.1 pad.14.clone
  2.3 0.7 add_add_fusion.buckets_ref
  3.0 0.7 stack.10
  3.7 0.7 stack.9
  4.3 0.1 copy.27
  4.5 0.6 pad.9.gains_ref
  5.1 1.3 pad.8.table_ref
  6.4 311.3 %shard_map.220 = (bf16[1472,512]{1,0:T(8,128)(2,1)}, bf16[1472,512]{1,0:T(8,128)(2,1)}, f32[8,1664]{1,0:T(8,128)}, bf16[184,384]{1,0:T(8,128)(2,1)}, bf16[184,38...) custom-call(bf16[1472,512]{1,0:T(8,128)(2,1)} %bitcast.20, ...), custom_call_target="tpu_custom_call" | custom-call | flops 57000001536 | bytes 100000000 | tf_op jit(solution)/shard_map/pallas_call | solution.py:1229
  317.7 1.4 fusion
  319.2 1.3 slice_bitcast_fusion
  320.4 0.0 copy-start.3
  320.4 3.2 convert_element_type.29
  323.7 0.0 copy-done.3
  323.7 0.0 copy-start.2
  323.7 1.8 convert_element_type.30
  325.5 0.0 copy-done.2
  325.5 0.0 copy-start.7
  325.5 0.0 copy-start.6
  325.5 0.0 copy-start.5
  325.5 0.0 copy-start.4
  325.5 1.8 convert_element_type.31
  327.3 0.0 copy-start.1
  327.3 0.0 copy-done.7
  327.3 0.7 convert_element_type.25
  328.0 0.0 copy-done.6
  328.0 0.7 convert_element_type.26
  328.7 0.0 copy-done.5
  328.7 0.7 convert_element_type.27
  329.5 0.0 copy-done.4
  329.5 0.7 convert_element_type.28
  330.2 0.0 copy-done.1
  330.2 0.0 copy-start
  330.2 1.1 copy.30
  331.3 0.8 copy-done
  332.1 1.1 copy.31
  (2 shorter events, 0.0 us)
Async XLA Ops:
  320.4 3.2 copy-start.3
  323.7 1.8 copy-start.2
  325.5 1.8 copy-start.7
  325.5 2.5 copy-start.6
  325.5 3.3 copy-start.5
  325.5 4.0 %copy-start.4 = (bf16[184,384]{1,0:T(8,128)(2,1)S(1)}, bf16[184,384]{1,0:T(8,128)(2,1)}, u32[]{:S(2)}) copy-start(bf16[184,384]{1,0:T(8,128)(2,1)} %get-tuple-element.28) | copy-start | bytes 423940
  327.3 2.9 copy-start.1
  330.2 1.9 copy-start

commit v2 on v1

--- a/solution.py
+++ b/solution.py
@@ -274,17 +274,17 @@
 
 HEAD_SLOTS = 7
 TAIL_SLOTS = 12
-HELPED = (1, 2, 4, 5)
+HELPED = (1, 2, 3, 4, 5, 6)
 SLOTS = {
-    "send": (0, 0, 1, 2, 2, 4, 6),
-    "forward": (1, 1, 5, 7, 8, 10, 16),
-    "swap": (2, 3, 7, 10, 11, 12, 18),
-    "get_forward": (2, 6, 11, 12, 14, 15, 18),
-    "get_swap": (5, 6, 11, 12, 14, 16, 19),
-    "turn": (10, 12, 15, 16, 18, 20, 23, 26, 28),
-    "rep": (13, 15, 16, 18, 21, 22, 24, 28, 30),
-    "mid": (15, 16, 18, 20, 22, 24, 25, 30, 31),
-    "last": (16, 18, 20, 22, 24, 25, 28, 31, 32),
+    "send": (0, 0, 0, 2, 2, 4, 4),
+    "forward": (1, 1, 1, 5, 5, 6, 7),
+    "swap": (4, 4, 4, 8, 10, 13, 15),
+    "get_forward": (3, 5, 5, 11, 12, 14, 16),
+    "get_swap": (3, 5, 5, 12, 14, 16, 17),
+    "turn": (10, 12, 14, 16, 19, 20, 24, 26, 27),
+    "rep": (12, 13, 16, 19, 22, 24, 25, 28, 29),
+    "mid": (14, 17, 19, 21, 24, 25, 27, 30, 31),
+    "last": (16, 19, 21, 24, 25, 27, 29, 31, 32),
 }
 
 
@@ -580,8 +580,7 @@
             ref[index, :, 0:w] = value
 
     def add_to(dst, i, src, j, w):
-        value = get(dst, i, w).astype(f32) + get(src, j, w).astype(f32)
-        put(dst, i, w, value.astype(bf16))
+        put(dst, i, w, get(dst, i, w) + get(src, j, w))
 
     def core_part(n, b, count, w):
         slot = n % 2
@@ -601,17 +600,20 @@
 
         def store(i):
             b = order[i][0]
-            return pltpu.make_async_copy(cut1(g, base + b, w), cut1(sum_ref, n * 8 + b, w), sum_sem.at[i])
+            return pltpu.make_async_copy(cut1(g, base + b, w), cut1(sum_ref, n * 8 + b, w), sum_sem.at[n, i])
 
         for i, (b, _, _) in enumerate(order):
             add_to(g, base + b, rc, slot * 8 + b, w)
             store(i).start()
-        for i, (b, dev, spot) in enumerate(order):
+        for i, (b, dev, spot) in enumerate(order[:4]):
             store(i).wait()
-            if dev is not None:
-                remote(
-                    cut1(sum_ref, n * 8 + b, w), cut1(hop_ref, n * 4 + spot, w), e1s.at[n], e1r.at[n, spot // 2], (dev, r)
-                ).start()
+            remote(
+                cut1(sum_ref, n * 8 + b, w), cut1(hop_ref, n * 4 + spot, w), e1s.at[n], e1r.at[n, spot // 2], (dev, r)
+            ).start()
+
+    def stored(n, w):
+        for i in range(4, 8):
+            settle(cut1(sum_ref, 0, w), sum_sem.at[n, i])
 
     def slot_free(n):
         settle(span(g, 0, 8, width_of(n)), e0s.at[n])
@@ -770,13 +772,13 @@
         ("forward", gathers(gather_forward, True)),
         ("send", lambda k: gather_send(("f", k))),
         ("turn", reduces(turn_start)),
+        ("rep", reduces(rep_start)),
         ("last", reduces(rep_last)),
         ("mid", reduces(rep_turn)),
         ("turn", reduces(turn_end)),
-        ("rep", reduces(rep_start)),
+        ("rep", reduces(rep_end)),
         ("get_forward", gathers(gather_forward, False)),
         ("get_swap", gathers(gather_swap, False)),
-        ("rep", reduces(rep_end)),
     )
     loop_at = HEAD_SLOTS
     tail_at = HEAD_SLOTS + 2 * chunks
@@ -982,31 +984,36 @@
 
     tok_tile = toks // 2
 
+    parts = [(half, k) for half in (0, 1) for k in (0, 1, 2)]
+    depth = 4
+
+    def load(t, p):
+        half, k = parts[p]
+        return pltpu.make_async_copy(
+            land_ref.at[pl.ds(t * 16 + half * 8, 8), :, pl.ds(k * sub, sub)],
+            wload.at[pl.ds((p % depth) * 8, 8)],
+            load_sem.at[p % depth],
+        )
+
+    def ffn_load(t):
+        for p in range(depth):
+            load(t, p).start()
+
     def ffn_chunk(t):
         slot = t % 2
-        parts = [(half, k) for half in (0, 1) for k in (0, 1, 2)]
-
-        def load(p):
-            half, k = parts[p]
-            return pltpu.make_async_copy(
-                land_ref.at[pl.ds(t * 16 + half * 8, 8), :, pl.ds(k * sub, sub)],
-                wload.at[pl.ds((p % 2) * 8, 8)],
-                load_sem.at[p % 2],
-            )
-
-        load(0).start()
         for p, (half, k) in enumerate(parts):
-            if p + 1 < len(parts):
-                load(p + 1).start()
-            load(p).wait()
+            load(t, p).wait()
             dst = (wg2, wu2, wd2)[k]
 
             @pl.loop(0, nbig)
             def _(i):
-                base = (p % 2) * 8 + 2 * i
+                base = (p % depth) * 8 + 2 * i
                 both = jnp.concatenate([wload[base].astype(f32), wload[base + 1].astype(f32)], axis=0)
                 sl = pl.ds(pl.multiple_of(i * big, 16), big)
                 dst[sl, half * sub : (half + 1) * sub] = both.astype(bf16)
+
+            if p + depth < len(parts):
+                load(t, p + depth).start()
 
         @pl.loop(0, toks // tok_tile)
         def _(m):
@@ -1041,9 +1048,11 @@
             core_part(t, 2 * i, 2, fw)
 
     def ffn_step(t, carry):
+        gather_done(("f", t))
+        ffn_load(t)
+        pl.when(t >= 1)(lambda: stored(t - 1, fw))
         do_in_loop(t, 0)
         pl.when(t >= 2)(lambda: slot_free(t - 2))
-        gather_done(("f", t))
         ffn_chunk(t)
         do_in_loop(t, 1)
         plane_send(t, fw)
@@ -1055,6 +1064,7 @@
 
     nv = chunks
     nq = chunks + 1
+    stored(nv - 1, fw)
     do(tail_at)
     pick = lax.broadcasted_iota(jnp.int32, (8, toks), 0)
 
@@ -1140,8 +1150,10 @@
     weight_grad(nq, 1, n1t, dkt)
     plane_send(nv, aw)
     core_part(nq, 0, 8, aw)
+    stored(nv, aw)
     do(tail_at + 4)
     plane_send(nq, aw)
+    stored(nq, aw)
     do(tail_at + 5)
 
     def first_back(i, acc):
@@ -1252,7 +1264,7 @@
             *([inner_rows] * 8),
             *([pltpu.VMEM((width, aw), bf16)] * 4),
             *([pltpu.VMEM((width, 2 * sub), bf16)] * 3),
-            pltpu.VMEM((16, rows, sub), bf16),
+            pltpu.VMEM((32, rows, sub), bf16),
             blocks(32),
             *([pltpu.VMEM((toks, 2 * sub), bf16)] * 3),
             blocks(16),
@@ -1267,9 +1279,9 @@
             dma(()),
             dma(()),
             *([dma((total,))] * 5),
-            dma((2,)),
+            dma((4,)),
             *([dma((total,))] * 2),
-            dma((8,)),
+            dma((total, 8)),
             dma((6,)),
             dma((total,)),
             dma((total, 2)),

time: 335 us -> 324 us (0.967)
  Pallas kernels: 311 us -> 301 us
    pallas_call x1, Pallas kernels: 311 us -> 301 us  [fused(): pl.pallas_call(functools.partial(fused_kernel, chunks=chunks, heads=heads...]
where the time goes in v2:
time: 324 us; the launch traced here: 322 us
  Pallas kernels  301 us (93%)
  other arithmetic  11.2 us (3%)
  local copies, waits for them, and re-layouts  10.1 us (3%)
    pallas_call x1, Pallas kernels, fused(): pl.pallas_call(functools.partial(fused_kernel, chunks=chunks, heads=heads...  301 us
    convert_element_type x7, other arithmetic, fused_body(): grads = [grad.astype(f32) for grad in grads[:7]]  9.72 us

profile of v2, /device:TPU:1, one launch (start us, length us, event | category | flops | bytes accessed | tf_op | source)
XLA Modules:
  0.0 322.5 jit_solution(17145542568904769571)
XLA Ops:
  0.6 0.8 reverse
  1.4 0.1 slice.15
  1.5 0.8 pad_add_fusion
  2.2 0.1 pad.14.clone
  2.3 0.7 add_add_fusion.buckets_ref
  3.0 0.7 stack.10
  3.7 0.7 stack.9
  4.3 0.1 copy.27
  4.5 0.6 pad.9.gains_ref
  5.1 1.3 pad.8.table_ref
  6.4 300.5 %shard_map.220 = (bf16[1472,512]{1,0:T(8,128)(2,1)}, bf16[1472,512]{1,0:T(8,128)(2,1)}, f32[8,1664]{1,0:T(8,128)}, bf16[184,384]{1,0:T(8,128)(2,1)}, bf16[184,38...) custom-call(bf16[1472,512]{1,0:T(8,128)(2,1)} %bitcast.20, ...), custom_call_target="tpu_custom_call" | custom-call | flops 57000001536 | bytes 100000000 | tf_op jit(solution)/shard_map/pallas_call | solution.py:1241
  306.9 1.4 fusion
  308.4 1.3 slice_bitcast_fusion
  309.6 0.0 copy-start.3
  309.6 3.2 convert_element_type.29
  312.9 0.0 copy-done.3
  312.9 0.0 copy-start.2
  312.9 1.8 convert_element_type.30
  314.7 0.0 copy-done.2
  314.7 0.0 copy-start.7
  314.7 0.0 copy-start.6
  314.7 0.0 copy-start.5
  314.7 0.0 copy-start.4
  314.7 1.8 convert_element_type.31
  316.5 0.0 copy-start.1
  316.5 0.0 copy-done.7
  316.5 0.7 convert_element_type.25
  317.2 0.0 copy-done.6
  317.2 0.7 convert_element_type.26
  317.9 0.0 copy-done.5
  317.9 0.7 convert_element_type.27
  318.7 0.0 copy-done.4
  318.7 0.7 convert_element_type.28
  319.4 0.0 copy-done.1
  319.4 0.0 copy-start
  319.4 1.1 copy.30
  320.5 0.8 copy-done
  321.3 1.1 copy.31
  (2 shorter events, 0.0 us)
Async XLA Ops:
  309.6 3.2 copy-start.3
  312.9 1.8 copy-start.2
  314.7 1.8 copy-start.7
  314.7 2.5 copy-start.6
  314.7 3.3 %copy-start.5 = (bf16[184,384]{1,0:T(8,128)(2,1)S(1)}, bf16[184,384]{1,0:T(8,128)(2,1)}, u32[]{:S(2)}) copy-start(bf16[184,384]{1,0:T(8,128)(2,1)} %get-tuple-element.27) | copy-start | bytes 423940
  314.7 4.0 %copy-start.4 = (bf16[184,384]{1,0:T(8,128)(2,1)S(1)}, bf16[184,384]{1,0:T(8,128)(2,1)}, u32[]{:S(2)}) copy-start(bf16[184,384]{1,0:T(8,128)(2,1)} %get-tuple-element.28) | copy-start | bytes 423940
  316.5 2.9 copy-start.1
  319.4 1.9 copy-start

commit v3 on v2

--- a/solution.py
+++ b/solution.py
@@ -273,18 +273,18 @@
     )
 
 HEAD_SLOTS = 7
-TAIL_SLOTS = 12
+TAIL_SLOTS = 14
 HELPED = (1, 2, 3, 4, 5, 6)
 SLOTS = {
-    "send": (0, 0, 0, 2, 2, 4, 4),
-    "forward": (1, 1, 1, 5, 5, 6, 7),
-    "swap": (4, 4, 4, 8, 10, 13, 15),
-    "get_forward": (3, 5, 5, 11, 12, 14, 16),
-    "get_swap": (3, 5, 5, 12, 14, 16, 17),
-    "turn": (10, 12, 14, 16, 19, 20, 24, 26, 27),
-    "rep": (12, 13, 16, 19, 22, 24, 25, 28, 29),
-    "mid": (14, 17, 19, 21, 24, 25, 27, 30, 31),
-    "last": (16, 19, 21, 24, 25, 27, 29, 31, 32),
+    "send": (0, 0, 0, 2, 2, 2, 2),
+    "forward": (1, 1, 1, 6, 7, 8, 11),
+    "swap": (2, 3, 4, 8, 10, 11, 17),
+    "get_forward": (1, 6, 7, 10, 11, 15, 16),
+    "get_swap": (3, 8, 9, 11, 13, 16, 18),
+    "turn": (10, 12, 15, 16, 20, 21, 24, 27, 29),
+    "rep": (13, 14, 19, 20, 23, 25, 26, 30, 31),
+    "mid": (17, 18, 20, 22, 24, 26, 29, 31, 32),
+    "last": (18, 21, 23, 24, 25, 28, 30, 32, 33),
 }
 
 
@@ -339,8 +339,6 @@
     vt,
     att,
     dat,
-    dqt,
-    dkt,
     dvt,
     wq,
     wk,
@@ -392,6 +390,7 @@
     sss,
     ssr,
     zcredit,
+    mcredit,
     *,
     chunks,
     heads,
@@ -666,54 +665,49 @@
             load.start()
 
     def rep_end(n, w):
-        slot = n % 2
-        if isinstance(n, int):
-            if n >= 2:
-                pl.when(outer)(functools.partial(rep_free, n))
-        else:
-            pl.when(outer & (n >= 2))(functools.partial(rep_free, n))
+        third = n % 3
+
+        def outer_room():
+            guarded(n, 3, lambda: pl.when(outer)(lambda: sent(vbuf, zis, n - 3)))
+            guarded(n, 2, lambda: pl.when(outer)(lambda: pl.semaphore_wait(zcredit, 1)))
+
+        outer_room()
         for load in rep_loads(n, w):
             load.wait()
-        for j in (0, 1):
+        for j in (c, 1 - c):
             value = get(stage_v, j, w).astype(f32) + get(stage_v, 2 + j, w).astype(f32)
             value = value + get(stage_v, 4 + j, w).astype(f32)
-            put(vbuf, slot * 2 + j, w, value.astype(bf16))
-
-        @pl.when(outer)
-        def _():
-            remote(
-                span(vbuf, slot * 2, 2, w), span(zi, slot * 2, 2, w), zis.at[n], zir.at[n], (s, mate)
-            ).start()
+            put(vbuf, third * 2 + j, w, value.astype(bf16))
+
+            @pl.when(outer)
+            def _():
+                remote(
+                    cut1(vbuf, third * 2 + j, w), cut1(zi, (n % 2) * 2 + j, w), zis.at[n, j], zir.at[n, j], (s, mate)
+                ).start()
+
+    def sent(ref, sems, n):
+        for j in (0, 1):
+            settle(cut1(ref, 0, width_of(n)), sems.at[n, j])
 
     def width_of(n):
         return fw if not isinstance(n, int) or n < chunks else aw
 
-    def rep_free(n):
-        earlier = n - 2
-        slot = n % 2
-        settle(span(vbuf, slot * 2, 2, width_of(earlier)), zis.at[earlier])
-        pl.semaphore_wait(zcredit, 1)
-
     def rep_turn(n, w):
-        slot = n % 2
+        third = n % 3
 
         @pl.when(inner)
         def _():
-            settle(span(zi, slot * 2, 2, w), zir.at[n])
-            for j in (0, 1):
-                add_to(vbuf, slot * 2 + j, zi, slot * 2 + j, w)
-
-            def credit():
-                pl.semaphore_signal(zcredit, inc=1, device_id=(s, mate), device_id_type=MESH)
-
-            if isinstance(n, int):
-                if n + 2 < total:
-                    credit()
-            else:
-                credit()
-            remote(
-                span(vbuf, slot * 2, 2, w), span(zm, slot * 2, 2, w), zms.at[n], zmr.at[n], (s, 3 - r)
-            ).start()
+            guarded(n, 3, lambda: pl.semaphore_wait(mcredit, 1))
+            for j in (c, 1 - c):
+                settle(cut1(zi, j, w), zir.at[n, j])
+                add_to(vbuf, third * 2 + j, zi, (n % 2) * 2 + j, w)
+                remote(
+                    cut1(vbuf, third * 2 + j, w), cut1(zm, third * 2 + j, w), zms.at[n, j], zmr.at[n, j], (s, 3 - r)
+                ).start()
+            guarded(total - 1 - n, 2, lambda: give_credit(zcredit, (s, mate)))
+
+    def give_credit(sem, dev):
+        pl.semaphore_signal(sem, inc=1, device_id=dev, device_id_type=MESH)
 
     def result(n, half, block):
         if isinstance(n, int) and n >= chunks:
@@ -731,35 +725,36 @@
 
     def rep_last(n, w):
         slot = n % 2
+        third = n % 3
 
         @pl.when(inner)
         def _():
-            settle(span(zm, slot * 2, 2, w), zmr.at[n])
-            if isinstance(n, int):
-                if n >= 2:
-                    u_free(n - 2, width_of(n - 2))
-            else:
-                pl.when(n >= 2)(lambda: u_free(n - 2, w))
-            for j in (0, 1):
-                value = get(vbuf, slot * 2 + j, w).astype(f32) + get(zm, slot * 2 + j, w).astype(f32)
+            guarded(n, 2, lambda: u_free(n - 2, width_of(n - 2)))
+
+            def both(j):
+                settle(cut1(zm, j, w), zmr.at[n, j])
+                value = get(vbuf, third * 2 + j, w).astype(f32) + get(zm, third * 2 + j, w).astype(f32)
                 put(ubuf, slot * 2 + j, w, value.astype(bf16))
-            keep = cut1(ubuf, slot * 2 + c, w)
-            give = cut1(ubuf, slot * 2 + 1 - c, w)
-
-            def finish(half):
-                for src, dst in result(n, half, keep):
+
+            def finish_keep(half):
+                for src, dst in result(n, half, cut1(ubuf, slot * 2 + c, w)):
                     remote(src, dst, us.at[n, 0], ur.at[n, half], (s, mate)).start()
                     pltpu.make_async_copy(src, dst, ul.at[n]).start()
-                for src, dst in result(n, half, give):
+
+            def finish_give(half):
+                for src, dst in result(n, half, cut1(ubuf, slot * 2 + 1 - c, w)):
                     remote(src, dst, us.at[n, 1], ur.at[n, half], (sc, mate)).start()
                     remote(src, dst, us.at[n, 2], ur.at[n, half], (sc, r)).start()
 
-            if w == fw:
-                finish(c)
-            else:
-                pl.when(c == 0)(lambda: finish(0))
-                pl.when(c == 1)(lambda: finish(1))
-            settle(span(vbuf, slot * 2, 2, w), zms.at[n])
+            for j, finish in ((c, finish_keep), (1 - c, finish_give)):
+                both(j)
+                if w == fw:
+                    finish(c)
+                else:
+                    pl.when(c == 0)(functools.partial(finish, 0))
+                    pl.when(c == 1)(functools.partial(finish, 1))
+            guarded(total - 1 - n, 3, lambda: give_credit(mcredit, (s, 3 - r)))
+            sent(vbuf, zms, n)
 
     def gathers(stage, mine):
         return lambda k: ahead(stage, k, mine)
@@ -1096,6 +1091,8 @@
     sms[0, :, 0:width] = token_sums(1)
     do(tail_at + 1)
 
+    dqt = dgt.at[pl.ds(0, aw)]
+    dkt = dup.at[pl.ds(0, aw)]
     dat[...] = dot_tn(wo[...], n2t[...]).astype(bf16)
 
     def weight_grad(n, half, left, right):
@@ -1189,8 +1186,8 @@
     small_send(0)
     for k in range(7, TAIL_SLOTS):
         do(tail_at + k)
-        for step in {7: (0,), 8: (1,), 9: (2, 3), 10: (4, 5)}.get(k, ()):
-            small_step(step)
+        if k < 13:
+            small_step(k - 7)
 
     settle(gland.at[pl.ds(0, 7)], gain_s)
     slot_free(nv)
@@ -1203,8 +1200,8 @@
 
     @pl.when(outer)
     def _():
-        for n in (nv, nq):
-            settle(span(vbuf, (n % 2) * 2, 2, aw), zis.at[n])
+        for n in (nv - 1, nv, nq):
+            sent(vbuf, zis, n)
         for n in range(total):
             for half in (0, 1):
                 settle(cut1(ubuf, 0, width_of(n)), ur.at[n, half])
@@ -1261,7 +1258,7 @@
             tok(f32),
             tok(f32),
             tok(f32),
-            *([inner_rows] * 8),
+            *([inner_rows] * 6),
             *([pltpu.VMEM((width, aw), bf16)] * 4),
             *([pltpu.VMEM((width, 2 * sub), bf16)] * 3),
             pltpu.VMEM((32, rows, sub), bf16),
@@ -1270,7 +1267,10 @@
             blocks(16),
             blocks(8),
             blocks(6),
-            *([blocks(4)] * 4),
+            blocks(6),
+            blocks(4),
+            blocks(6),
+            blocks(4),
             pltpu.VMEM((8, lanes), f32),
             pltpu.VMEM((128, lanes), bf16),
             pltpu.VMEM((8, lanes), f32),
@@ -1285,12 +1285,14 @@
             dma((6,)),
             dma((total,)),
             dma((total, 2)),
-            *([dma((total,))] * 6),
+            *([dma((total,))] * 2),
+            *([dma((total, 2))] * 4),
             dma((total, 3)),
             dma((total,)),
             dma((total, 2)),
             dma((6,)),
             dma((6,)),
+            pltpu.SemaphoreType.REGULAR,
             pltpu.SemaphoreType.REGULAR,
         ],
         compiler_params=pltpu.CompilerParams(

time: 324 us -> 317 us (0.978)
  Pallas kernels: 301 us -> 294 us
    pallas_call x1, Pallas kernels: 301 us -> 294 us  [fused(): pl.pallas_call(functools.partial(fused_kernel, chunks=chunks, heads=heads...]
where the time goes in v3:
time: 317 us; the launch traced here: 316 us
  Pallas kernels  294 us (93%)
  other arithmetic  11.2 us (4%)
  local copies, waits for them, and re-layouts  10.1 us (3%)
    pallas_call x1, Pallas kernels, fused(): pl.pallas_call(functools.partial(fused_kernel, chunks=chunks, heads=heads...  294 us
    convert_element_type x7, other arithmetic, fused_body(): grads = [grad.astype(f32) for grad in grads[:7]]  9.72 us

profile of v3, /device:TPU:1, one launch (start us, length us, event | category | flops | bytes accessed | tf_op | source)
XLA Modules:
  0.0 315.5 jit_solution(17472671391063482662)
XLA Ops:
  0.6 0.8 reverse
  1.4 0.1 slice.15
  1.5 0.8 pad_add_fusion
  2.2 0.1 pad.14.clone
  2.3 0.7 add_add_fusion.buckets_ref
  3.0 0.7 stack.10
  3.7 0.7 stack.9
  4.3 0.1 copy.27
  4.5 0.6 pad.9.gains_ref
  5.1 1.3 pad.8.table_ref
  6.4 293.6 %shard_map.220 = (bf16[1472,512]{1,0:T(8,128)(2,1)}, bf16[1472,512]{1,0:T(8,128)(2,1)}, f32[8,1664]{1,0:T(8,128)}, bf16[184,384]{1,0:T(8,128)(2,1)}, bf16[184,38...) custom-call(bf16[1472,512]{1,0:T(8,128)(2,1)} %bitcast.20, ...), custom_call_target="tpu_custom_call" | custom-call | flops 57000001536 | bytes 100000000 | tf_op jit(solution)/shard_map/pallas_call | solution.py:1238
  300.0 1.4 fusion
  301.5 1.3 slice_bitcast_fusion
  302.7 0.0 copy-start.3
  302.7 3.2 %convert_element_type.29 = f32[184,3584]{1,0:T(8,128)} convert(bf16[184,3584]{1,0:T(8,128)(2,1)} %get-tuple-element.29) | non-fusion elementwise | flops 659456 | bytes 3956736 | tf_op jit(solution)/shard_map/convert_element_type | solution.py:1324
  305.9 0.0 copy-done.3
  305.9 0.0 copy-start.2
  305.9 1.8 convert_element_type.30
  307.7 0.0 copy-done.2
  307.7 0.0 copy-start.7
  307.7 0.0 copy-start.6
  307.8 0.0 copy-start.5
  307.8 0.0 copy-start.4
  307.8 1.8 convert_element_type.31
  309.6 0.0 copy-start.1
  309.6 0.0 copy-done.7
  309.6 0.7 convert_element_type.25
  310.3 0.0 copy-done.6
  310.3 0.7 convert_element_type.26
  311.0 0.0 copy-done.5
  311.0 0.7 convert_element_type.27
  311.8 0.0 copy-done.4
  311.8 0.7 convert_element_type.28
  312.5 0.0 copy-done.1
  312.5 0.0 copy-start
  312.5 1.1 copy.30
  313.6 0.8 copy-done
  314.4 1.1 copy.31
  (2 shorter events, 0.0 us)
Async XLA Ops:
  302.7 3.2 %copy-start.3 = (bf16[184,3584]{1,0:T(8,128)(2,1)S(1)}, bf16[184,3584]{1,0:T(8,128)(2,1)}, u32[]{:S(2)}) copy-start(bf16[184,3584]{1,0:T(8,128)(2,1)} %get-tuple-element.30) | copy-start | bytes 3956740
  305.9 1.8 copy-start.2
  307.7 1.8 copy-start.7
  307.7 2.5 copy-start.6
  307.8 3.3 %copy-start.5 = (bf16[184,384]{1,0:T(8,128)(2,1)S(1)}, bf16[184,384]{1,0:T(8,128)(2,1)}, u32[]{:S(2)}) copy-start(bf16[184,384]{1,0:T(8,128)(2,1)} %get-tuple-element.27) | copy-start | bytes 423940
  307.8 4.0 %copy-start.4 = (bf16[184,384]{1,0:T(8,128)(2,1)S(1)}, bf16[184,384]{1,0:T(8,128)(2,1)}, u32[]{:S(2)}) copy-start(bf16[184,384]{1,0:T(8,128)(2,1)} %get-tuple-element.28) | copy-start | bytes 423940
  309.6 2.9 copy-start.1
  312.5 1.9 copy-start

commit v4 on v3

--- a/solution.py
+++ b/solution.py
@@ -889,10 +889,13 @@
     ssum = jnp.sum(over_rows(square_sum, zero8), axis=0, keepdims=True)
     r1 = lax.rsqrt(ssum * (1.0 / width) + eps)
 
-    bucket_index = lax.broadcasted_iota(jnp.int32, (table_ref.shape[1], lanes), 0)
-    rev_hot = (bucket_index == buckets_ref[0:1, :]).astype(bf16)
-    onehot[...] = (bucket_index == buckets_ref[1:2, :]).astype(bf16)
-    revb[...] = dot_nn(table_ref[...], rev_hot)
+    bucket_index = lax.broadcasted_iota(jnp.int32, onehot.shape, 0)
+    onehot[...] = (bucket_index == buckets_ref[...]).astype(bf16)
+    turn_index = lax.broadcasted_iota(jnp.int32, (toks, toks), 0) + lax.broadcasted_iota(jnp.int32, (toks, toks), 1)
+    flip = (turn_index == toks - 1).astype(bf16)
+    offset_bias = dot_nn(table_ref[...], onehot[0 : table_ref.shape[1], :]).astype(bf16)
+    revb[0:heads, 0:toks] = dot_nn(offset_bias[:, toks:lanes], flip)
+    revb[0:heads, toks:lanes] = dot_nn(offset_bias[:, 0:toks], flip)
 
     settle(gland.at[pl.ds(0, 7)], gain_r)
     settle(gland.at[0], load_sem.at[1])
@@ -942,7 +945,7 @@
         keys = half_tok * (block + 1)
         low = half_tok * block
         row = jnp.broadcast_to(revb[pl.ds(h, 1), :], (half_tok, lanes))
-        bias = pltpu.roll(row, (low + 1 - toks) % lanes, 1, stride=1, stride_axis=0)[:, :keys]
+        bias = pltpu.roll(row, (low - toks) % lanes, 1, stride=1, stride_axis=0)[:, :keys]
         scores = dot_tn(qt[head, low : low + half_tok], kt[head, 0:keys]) + bias
         e = jnp.exp(scores - jnp.max(scores, axis=1, keepdims=True))
         return e * (1.0 / jnp.sum(e, axis=1, keepdims=True)), low, keys
@@ -1106,11 +1109,7 @@
     slot_free(5)
     weight_grad(nv, 1, n2t, att)
     do(tail_at + 2)
-    flip = (
-        lax.broadcasted_iota(jnp.int32, (toks, toks), 0) + lax.broadcasted_iota(jnp.int32, (toks, toks), 1)
-        == toks - 1
-    )
-    hid[...] = flip.astype(bf16)
+    hid[...] = (turn_index == toks - 1).astype(bf16)
     doff[...] = jnp.zeros(doff.shape, f32)
 
     def attend_back(h, carry):
@@ -1225,10 +1224,7 @@
     total = chunks + 2
     lanes = 2 * toks
     small_lanes = (width + 127) // 128 * 128 + 128
-    padded = jnp.concatenate([buckets, jnp.full((1,), -1, jnp.int32)])
-    turned = jnp.concatenate([buckets[::-1], jnp.full((1,), -1, jnp.int32)])
-    bucket_rows = jnp.concatenate([turned[None], padded[None], jnp.full((6, lanes), -1, jnp.int32)])
-    table = jnp.pad(bias_table.T, ((0, 8 - heads), (0, 128 - bias_table.shape[0])))
+    bucket_rows = jnp.pad(buckets, (0, 1), constant_values=-1)[None]
     vm = pl.BlockSpec(memory_space=pltpu.VMEM)
     hbm = pl.BlockSpec(memory_space=pltpu.HBM)
     dma = pltpu.SemaphoreType.DMA
@@ -1299,7 +1295,33 @@
             collective_id=0, has_side_effects=True, vmem_limit_bytes=60 * 2**20
         ),
         cost_estimate=pl.CostEstimate(flops=57 * 10**9, bytes_accessed=10**8, transcendentals=10**7),
-    )(tokens.T, cotangent.T, bucket_rows, table, gains, *weights)
+    )(tokens.T, cotangent.T, bucket_rows, bias_table.T, gains, *weights)
+
+
+def widen_kernel(*refs):
+    count = len(refs) // 2
+    for src, dst in zip(refs[:count], refs[count:]):
+        dst[...] = src[...].astype(dst.dtype)
+
+
+def widen(out, gtok, grads):
+    steps = 4
+    width, toks = out.shape
+    rows, ff = grads[-1].shape
+    act = pl.BlockSpec((width // steps, toks), lambda i: (i, 0))
+    small = pl.BlockSpec(grads[0].shape, lambda i: (0, 0))
+    large = pl.BlockSpec((rows, ff // steps), lambda i: (0, i))
+    specs = [act] * 2 + [small] * 4 + [large] * 3
+    return pl.pallas_call(
+        widen_kernel,
+        grid=(steps,),
+        out_shape=[jax.ShapeDtypeStruct(v.shape, bf16) for v in (out, gtok)]
+        + [jax.ShapeDtypeStruct(v.shape, f32) for v in grads],
+        in_specs=specs,
+        out_specs=specs,
+        compiler_params=pltpu.CompilerParams(vmem_limit_bytes=60 * 2**20),
+        cost_estimate=pl.CostEstimate(flops=10**7, bytes_accessed=2 * 10**7, transcendentals=0),
+    )(out, gtok, *grads)
 
 
 def fused_body(
@@ -1318,10 +1340,11 @@
     w_down,
 ):
     rows = w_query.shape[0]
-    gains = jnp.pad(jnp.stack([attn_gain, ffn_gain], axis=1), ((0, 0), (0, 126)))
+    lane = lax.broadcasted_iota(jnp.int32, (rows, 128), 1)
+    gains = jnp.where(lane == 0, attn_gain[:, None], ffn_gain[:, None])
     weights = (w_query, w_key, w_value, w_output, w_gate, w_up, w_down)
     out, gtok, small, *grads = fused(tokens, cotangent, buckets, bias_table, gains, weights)
-    grads = [grad.astype(f32) for grad in grads[:7]]
+    out, gtok, *grads = widen(out, gtok, grads[:7])
     own = lax.dynamic_slice(small, (0, lax.axis_index("shard") * rows), (2, rows))
     table = small[0 : bias_table.shape[1], small.shape[1] - 128 :][:, 0 : bias_table.shape[0]].T
     return (out.T, gtok.T, own[0], *grads[:4], own[1], *grads[4:], table)

time: 317 us -> 308 us (0.972)
  other arithmetic: 11.2 us -> 1.42 us
  Pallas kernels: 294 us -> 301 us
  local copies, waits for them, and re-layouts: 10.1 us -> 3.98 us
    convert_element_type x7 -> x0, other arithmetic: 9.72 us -> none  [fused_body(): grads = [grad.astype(f32) for grad in grads[:7]]]
    pallas_call x0 -> x1, Pallas kernels: none -> 7.66 us  [widen(): pl.pallas_call(widen_kernel, grid=(steps,), out_shape=[jax.ShapeDtypeStru...]
    unnamed x20 -> x0, local copies, waits for them, and re-layouts: 3.91 us -> none
where the time goes in v4:
time: 308 us; the launch traced here: 307 us
  Pallas kernels  301 us (98%)
  local copies, waits for them, and re-layouts  3.98 us (1%)
    pallas_call x1, Pallas kernels, fused(): pl.pallas_call(functools.partial(fused_kernel, chunks=chunks, heads=heads...  294 us
    pallas_call x1, Pallas kernels, widen(): pl.pallas_call(widen_kernel, grid=(steps,), out_shape=[jax.ShapeDtypeStru...  7.66 us

profile of v4, /device:TPU:1, one launch (start us, length us, event | category | flops | bytes accessed | tf_op | source)
XLA Modules:
  0.0 307.3 jit_solution(4252565602974512192)
XLA Ops:
  0.7 1.4 broadcast_select_fusion.gains_ref
  2.1 1.3 pad.4
  3.3 293.5 %shard_map.220 = (bf16[1472,512]{1,0:T(8,128)(2,1)}, bf16[1472,512]{1,0:T(8,128)(2,1)}, f32[8,1664]{1,0:T(8,128)}, bf16[184,384]{1,0:T(8,128)(2,1)}, bf16[184,38...) custom-call(bf16[1472,512]{1,0:T(8,128)(2,1)} %bitcast.13, ...), custom_call_target="tpu_custom_call" | custom-call | flops 57000001536 | bytes 100000000 | tf_op jit(solution)/shard_map/pallas_call | solution.py:1234
  296.9 7.7 %shard_map.221 = (bf16[1472,512]{1,0:T(8,128)(2,1)}, bf16[1472,512]{1,0:T(8,128)(2,1)}, f32[184,384]{1,0:T(8,128)}, f32[184,384]{1,0:T(8,128)}, f32[184,384]{1,0...) custom-call(bf16[1472,512]{1,0:T(8,128)(2,1)} %get-tuple-element.31.refs_0_, ...), custom_call_target="tpu_custom_call" | custom-call | flops 10000000 | bytes 20000000 | tf_op jit(solution)/shard_map/pallas_call | solution.py:1315
  304.6 1.4 fusion
  306.0 1.3 slice_bitcast_fusion
  (1 shorter events, 0.0 us)

commit v5 on v4

--- a/solution.py
+++ b/solution.py
@@ -1300,11 +1300,14 @@
 
 def widen_kernel(*refs):
     count = len(refs) // 2
-    for src, dst in zip(refs[:count], refs[count:]):
+    for src, dst in zip(refs[: count - 1], refs[count:-1]):
         dst[...] = src[...].astype(dst.dtype)
-
-
-def widen(out, gtok, grads):
+    sums, table = refs[count - 1], refs[-1]
+    lane = sums.shape[1] - 128
+    table[...] = sums[0 : table.shape[0], lane : lane + table.shape[1]]
+
+
+def widen(out, gtok, grads, sums, table_shape):
     steps = 4
     width, toks = out.shape
     rows, ff = grads[-1].shape
@@ -1312,16 +1315,18 @@
     small = pl.BlockSpec(grads[0].shape, lambda i: (0, 0))
     large = pl.BlockSpec((rows, ff // steps), lambda i: (0, i))
     specs = [act] * 2 + [small] * 4 + [large] * 3
+    whole = lambda shape: pl.BlockSpec(shape, lambda i: (0, 0))
     return pl.pallas_call(
         widen_kernel,
         grid=(steps,),
         out_shape=[jax.ShapeDtypeStruct(v.shape, bf16) for v in (out, gtok)]
-        + [jax.ShapeDtypeStruct(v.shape, f32) for v in grads],
-        in_specs=specs,
-        out_specs=specs,
+        + [jax.ShapeDtypeStruct(v.shape, f32) for v in grads]
+        + [jax.ShapeDtypeStruct(table_shape, f32)],
+        in_specs=specs + [whole(sums.shape)],
+        out_specs=specs + [whole(table_shape)],
         compiler_params=pltpu.CompilerParams(vmem_limit_bytes=60 * 2**20),
         cost_estimate=pl.CostEstimate(flops=10**7, bytes_accessed=2 * 10**7, transcendentals=0),
-    )(out, gtok, *grads)
+    )(out, gtok, *grads, sums)
 
 
 def fused_body(
@@ -1344,10 +1349,9 @@
     gains = jnp.where(lane == 0, attn_gain[:, None], ffn_gain[:, None])
     weights = (w_query, w_key, w_value, w_output, w_gate, w_up, w_down)
     out, gtok, small, *grads = fused(tokens, cotangent, buckets, bias_table, gains, weights)
-    out, gtok, *grads = widen(out, gtok, grads[:7])
+    out, gtok, *grads, table = widen(out, gtok, grads[:7], small, bias_table.shape[::-1])
     own = lax.dynamic_slice(small, (0, lax.axis_index("shard") * rows), (2, rows))
-    table = small[0 : bias_table.shape[1], small.shape[1] - 128 :][:, 0 : bias_table.shape[0]].T
-    return (out.T, gtok.T, own[0], *grads[:4], own[1], *grads[4:], table)
+    return (out.T, gtok.T, own[0], *grads[:4], own[1], *grads[4:], table.T)
 
 
 def solution(mesh):

time: 308 us -> 307 us (level)
  no operation moved by 1% of the time
where the time goes in v5:
time: 307 us; the launch traced here: 306 us
  Pallas kernels  301 us (98%)
    pallas_call x1, Pallas kernels, fused(): pl.pallas_call(functools.partial(fused_kernel, chunks=chunks, heads=heads...  294 us
    pallas_call x1, Pallas kernels, widen(): pl.pallas_call(widen_kernel, grid=(steps,), out_shape=[jax.ShapeDtypeStru...  7.91 us

profile of v5, /device:TPU:1, one launch (start us, length us, event | category | flops | bytes accessed | tf_op | source)
XLA Modules:
  0.0 306.2 jit_solution(11915345921949897424)
XLA Ops:
  0.7 1.4 broadcast_select_fusion.gains_ref
  2.1 1.3 pad.4
  3.3 293.5 %shard_map.220 = (bf16[1472,512]{1,0:T(8,128)(2,1)}, bf16[1472,512]{1,0:T(8,128)(2,1)}, f32[8,1664]{1,0:T(8,128)}, bf16[184,384]{1,0:T(8,128)(2,1)}, bf16[184,38...) custom-call(bf16[1472,512]{1,0:T(8,128)(2,1)} %bitcast.12, ...), custom_call_target="tpu_custom_call" | custom-call | flops 57000001536 | bytes 100000000 | tf_op jit(solution)/shard_map/pallas_call | solution.py:1234
  296.9 7.9 %shard_map.221 = (bf16[1472,512]{1,0:T(8,128)(2,1)}, bf16[1472,512]{1,0:T(8,128)(2,1)}, f32[184,384]{1,0:T(8,128)}, f32[184,384]{1,0:T(8,128)}, f32[184,384]{1,0...) custom-call(bf16[1472,512]{1,0:T(8,128)(2,1)} %get-tuple-element.32., ...), custom_call_target="tpu_custom_call" | custom-call | flops 10000000 | bytes 20000000 | tf_op jit(solution)/shard_map/pallas_call | solution.py:1319
  304.8 1.4 fusion
  (1 shorter events, 0.0 us)
